TPU v7x, 1024 devices: a whole 4x4x32 slice. The times are simulated.
1024 devices in a mesh: section: 4 (over x), dp: 16 (over z_lo), expert: 16 (over y, z_hi, core).
Axes of the slice: x: 4, y: 4, z: 32 (z_hi: 2, z_lo: 16; z = z_hi * 16 + z_lo), core: 2. Of those that a mesh axis runs over, the one named last changes fastest.
Arguments:
- tokens: bfloat16 [4, 6144, 1024], P('section', ('dp', 'expert')), may hold values from -24 to 24
- routes: int32 [4, 6144, 6], P('section', ('dp', 'expert')), may hold values from 0 to 31, all different within a row; in each aligned block of 24 rows (0 to 23, 24 to 47, ..., all dimensions but the last counted through in order) at most 6 rows name the same one
- gate_values: float32 [4, 6144, 6], P('section', ('dp', 'expert')), may hold values from 0.1 to 1
- up_weight: bfloat16 [4, 32, 1024, 704], P('section', 'expert'), may hold values from -0.1875 to 0.1875
- down_weight: bfloat16 [4, 32, 704, 1024], P('section', 'expert'), may hold values from -0.21875 to 0.21875
- out_grad: bfloat16 [4, 6144, 1024], P('section', ('dp', 'expert')), may hold values from -6 to 6
Outputs:
- layer_output: bfloat16 [4, 6144, 1024], P('section', ('dp', 'expert'))
- sent_grad: bfloat16 [4, 6144, 1024], P('section', ('dp', 'expert'))
- gate_grad: float32 [4, 6144, 6], P('section', ('dp', 'expert'))
- up_grad: bfloat16 [4, 32, 1024, 704], P('section', 'expert', 'dp')
- down_grad: bfloat16 [4, 32, 1024, 704], P('section', 'expert', 'dp')
Inputs may be any that keep to these rules, and one draw needn't show every extreme that they name: `routes`: each token names 6 different experts. Within one layer, the 24 tokens of one device name no expert more than 6 times, and some device names some expert exactly 6 times.
All inputs are finite; a program needn't handle non-finite values.
Results may differ from a plain program's by a relative error of at most 0.022.
Values may be sent and summed in bfloat16 or wider, within the bound.
No kernel may reach another device: no remote copies, remote signals or barrier semaphores. Data moves between devices by JAX's collectives and lax.ppermute only.
A program may use at most 64 MiB of HBM per device.

v0:
```python
import jax
import jax.numpy as jnp
from jax import lax
from jax.sharding import PartitionSpec as P


def from_behind(block, axis, distance):
    devices = range(lax.axis_size(axis))
    route = [((i - distance) % len(devices), i) for i in devices]
    return lax.ppermute(block, axis, route)


def silu_slope(hidden):
    logistic = jax.nn.sigmoid(hidden)
    return logistic * (1.0 + hidden * (1.0 - logistic))


def slot_table(route_rows, experts_all, capacity):
    matches = (route_rows[:, None] == jnp.arange(experts_all, dtype=jnp.int32)[None, :]).astype(
        jnp.int32
    )
    counts = jnp.cumsum(matches, axis=0)
    within = jnp.sum(matches * counts, axis=1) - 1
    target = route_rows * capacity + within
    return (target[:, None] == jnp.arange(experts_all * capacity, dtype=jnp.int32)[None, :]).astype(
        jnp.bfloat16
    )


def to_experts(stacked):
    return lax.all_to_all(stacked, "expert", split_axis=0, concat_axis=0, tiled=True)


def from_experts(stacked):
    return lax.all_to_all(stacked, "expert", split_axis=0, concat_axis=0, tiled=True)


def expert_forward(arrived_inputs, up_local, down_local):
    hidden = jnp.einsum(
        "secd,edh->sech", arrived_inputs, up_local, preferred_element_type=jnp.float32
    )
    activated = jax.nn.silu(hidden).astype(jnp.bfloat16)
    produced = jnp.einsum(
        "sech,ehd->secd", activated, down_local, preferred_element_type=jnp.float32
    ).astype(jnp.bfloat16)
    return (hidden, activated, produced)


def expert_backward(arrived_grads, hidden, up_local, down_local):
    act_grad = jnp.einsum(
        "secd,ehd->sech", arrived_grads, down_local, preferred_element_type=jnp.float32
    )
    hidden_grad = (act_grad * silu_slope(hidden)).astype(jnp.bfloat16)
    input_rows = jnp.einsum(
        "sech,edh->secd", hidden_grad, up_local, preferred_element_type=jnp.float32
    ).astype(jnp.bfloat16)
    return (hidden_grad, input_rows)


def weight_term(row_side, unit_side):
    return jnp.einsum("secd,sech->edh", row_side, unit_side, preferred_element_type=jnp.float32)


def body(tokens, routes, gate_values, up_weight, down_weight, out_grad):
    token_rows = tokens[0]
    route_rows = routes[0].reshape(-1)
    gate_rows = gate_values[0]
    grad_rows = out_grad[0]
    up_local = up_weight[0]
    down_local = down_weight[0]
    local_experts = up_local.shape[0]
    groups = lax.axis_size("expert")
    experts_all = local_experts * groups
    tok_count = token_rows.shape[0]
    top_count = routes.shape[2]
    feature_count = token_rows.shape[1]
    capacity = min(
        tok_count, (7 * tok_count * top_count + 6 * experts_all - 1) // (6 * experts_all)
    )
    placing = slot_table(route_rows, experts_all, capacity)
    by_token = jnp.sum(placing.reshape(tok_count, top_count, -1), axis=1)
    slot_shape = (groups, local_experts, capacity, feature_count)
    sent_inputs = (
        jnp.einsum("ts,td->sd", by_token, token_rows, preferred_element_type=jnp.float32)
        .astype(jnp.bfloat16)
        .reshape(slot_shape)
    )
    grad_float = grad_rows.astype(jnp.float32)
    scaled = (
        (gate_rows[:, :, None] * grad_float[:, None, :])
        .astype(jnp.bfloat16)
        .reshape(tok_count * top_count, feature_count)
    )
    sent_grads = (
        jnp.einsum("rs,rd->sd", placing, scaled, preferred_element_type=jnp.float32)
        .astype(jnp.bfloat16)
        .reshape(slot_shape)
    )
    arrived_inputs = to_experts(sent_inputs[:, None])[:, 0]
    hidden, activated, produced = expert_forward(arrived_inputs, up_local, down_local)
    came_back = from_experts(produced[:, None])[:, 0]
    arrived_grads = to_experts(sent_grads[:, None])[:, 0]
    hidden_grad, input_rows = expert_backward(arrived_grads, hidden, up_local, down_local)
    rows_back = from_experts(input_rows[:, None])[:, 0]
    back_flat = came_back.reshape(-1, feature_count)
    picked = jnp.einsum(
        "rs,sd->rd", placing, back_flat, preferred_element_type=jnp.float32
    ).reshape(tok_count, top_count, feature_count)
    layer_output = jnp.sum(gate_rows[:, :, None] * picked, axis=1).astype(jnp.bfloat16)
    gate_grad = jnp.sum(grad_float[:, None, :] * picked, axis=2)
    grads_back = jnp.einsum(
        "rs,sd->rd",
        placing,
        rows_back.reshape(-1, feature_count),
        preferred_element_type=jnp.float32,
    )
    input_grad = jnp.sum(grads_back.reshape(tok_count, top_count, feature_count), axis=1).astype(
        jnp.bfloat16
    )
    sent_back = from_behind(input_grad, "section", -1)
    up_sum, down_sum = (
        lax.psum_scatter(
            weight_term(arrived_inputs, hidden_grad).astype(jnp.bfloat16),
            "dp",
            scatter_dimension=1,
            tiled=True,
        ).astype(jnp.float32),
        lax.psum_scatter(
            weight_term(arrived_grads, activated).astype(jnp.bfloat16),
            "dp",
            scatter_dimension=1,
            tiled=True,
        ).astype(jnp.float32),
    )
    return (
        layer_output[None],
        sent_back[None],
        gate_grad[None],
        up_sum.astype(jnp.bfloat16)[None],
        down_sum.astype(jnp.bfloat16)[None],
    )


def solution(mesh):
    placed = (
        P("section", ("dp", "expert"), None),
        P("section", ("dp", "expert"), None),
        P("section", ("dp", "expert"), None),
        P("section", "expert", None, None),
        P("section", "expert", None, None),
        P("section", ("dp", "expert"), None),
    )
    return jax.shard_map(
        body,
        mesh=mesh,
        in_specs=placed,
        out_specs=(
            P("section", ("dp", "expert"), None),
            P("section", ("dp", "expert"), None),
            P("section", ("dp", "expert"), None),
            P("section", "expert", "dp", None),
            P("section", "expert", "dp", None),
        ),
        check_vma=False,
    )
```

profile of v0, /device:TPU:24, one launch (start us, length us, event | category | flops | bytes accessed | tf_op | source)
XLA Modules:
  0.0 586.7 jit_solution(9261796324224313550)
XLA Ops:
  7.2 0.9 copy.53
  9.5 1.8 convolution_convert_fusion.1
  11.3 1.1 broadcast_in_dim_reshape.6
  12.4 1.2 copy.59
  13.6 31.2 %all-to-all-start = ((bf16[16,1,2,6,1024]{4,2,3,1,0:T(2,128)(2,1)}), bf16[16,1,2,6,1024]{4,2,3,1,0:T(2,128)(2,1)}, u32[]{:S(2)}, u32[]{:S(2)}) async-start(bf16[16,1,2,6,1024]{4,2,3,1,0:T(2,128)(2,1)} %copy.59), calls=%async_computation | async-start | bytes 786432 | tf_op jit(solution)/shard_map/all_to_all | solution.py:31
  45.7 1.0 mul.80.clone
  46.6 1.2 mul.81
  47.8 1.1 convolution_convert_fusion
  49.0 1.1 broadcast_in_dim_reshape.7
  50.1 1.1 copy.65
  51.3 20.3 %all-to-all-done = bf16[16,1,2,6,1024]{4,2,3,1,0:T(2,128)(2,1)} async-done(((bf16[16,1,2,6,1024]{4,2,3,1,0:T(2,128)(2,1)}), bf16[16,1,2,6,1024]{4,2,3,1,0:T(2,128)(2,1)}, u32[]{:S(2)}, u32[]{:S(2)}) %all-to-all-start) | async-done | bytes 393248 | tf_op jit(solution)/shard_map/all_to_all | solution.py:31
  71.6 6.4 %all-to-all-start.2 = ((bf16[16,1,2,6,1024]{4,2,3,1,0:T(2,128)(2,1)}), bf16[16,1,2,6,1024]{4,2,3,1,0:T(2,128)(2,1)}, u32[]{:S(2)}, u32[]{:S(2)}) async-start(bf16[16,1,2,6,1024]{4,2,3,1,0:T(2,128)(2,1)} %copy.65), calls=%async_computation.2 | async-start | bytes 786432 | tf_op jit(solution)/shard_map/all_to_all | solution.py:31
  78.0 2.9 fusion.17
  81.0 22.7 %all-to-all-done.2 = bf16[16,1,2,6,1024]{4,2,3,1,0:T(2,128)(2,1)} async-done(((bf16[16,1,2,6,1024]{4,2,3,1,0:T(2,128)(2,1)}), bf16[16,1,2,6,1024]{4,2,3,1,0:T(2,128)(2,1)}, u32[]{:S(2)}, u32[]{:S(2)}) %all-to-all-start.2) | async-done | bytes 393248 | tf_op jit(solution)/shard_map/all_to_all | solution.py:31
  103.7 3.7 bitcast_convert_fusion
  108.0 1.2 copy.61
  109.2 14.8 %all-to-all-start.1 = ((bf16[16,1,2,6,1024]{4,2,3,1,0:T(2,128)(2,1)}), bf16[16,1,2,6,1024]{4,2,3,1,0:T(2,128)(2,1)S(1)}, u32[]{:S(2)}, u32[]{:S(2)}) async-start(bf16[16,1,2,6,1024]{4,2,3,1,0:T(2,128)(2,1)} %copy.61), calls=%async_computation.1 | async-start | bytes 786432 | tf_op jit(solution)/shard_map/all_to_all | solution.py:35
  124.0 2.2 fusion.23
  126.9 3.7 bitcast_convert_fusion.1
  130.7 2.5 fusion.26
  133.2 1.2 copy.67
  134.4 15.1 %all-to-all-done.1 = bf16[16,1,2,6,1024]{4,2,3,1,0:T(2,128)(2,1)S(1)} async-done(((bf16[16,1,2,6,1024]{4,2,3,1,0:T(2,128)(2,1)}), bf16[16,1,2,6,1024]{4,2,3,1,0:T(2,128)(2,1)S(1)}, u32[]{:S(2)}, u32[]{:S(2)}) %all-to-all-start.1) | async-done | bytes 393248 | tf_op jit(solution)/shard_map/all_to_all | solution.py:35
  149.4 11.8 %all-to-all-start.3 = ((bf16[16,1,2,6,1024]{4,2,3,1,0:T(2,128)(2,1)}), bf16[16,1,2,6,1024]{4,2,3,1,0:T(2,128)(2,1)}, u32[]{:S(2)}, u32[]{:S(2)}) async-start(bf16[16,1,2,6,1024]{4,2,3,1,0:T(2,128)(2,1)} %copy.67), calls=%async_computation.3 | async-start | bytes 786432 | tf_op jit(solution)/shard_map/all_to_all | solution.py:35
  161.2 1.1 copy.62
  162.3 0.9 reshape.111
  163.2 30.4 %all-to-all-done.3 = bf16[16,1,2,6,1024]{4,2,3,1,0:T(2,128)(2,1)} async-done(((bf16[16,1,2,6,1024]{4,2,3,1,0:T(2,128)(2,1)}), bf16[16,1,2,6,1024]{4,2,3,1,0:T(2,128)(2,1)}, u32[]{:S(2)}, u32[]{:S(2)}) %all-to-all-start.3) | async-done | bytes 393248 | tf_op jit(solution)/shard_map/all_to_all | solution.py:35
  193.6 1.1 copy.68
  195.6 1.2 convolution_reduce_fusion
  196.9 4.8 collective-permute-start
  201.7 2.0 multiply_reduce_fusion
  204.3 168.0 %reduce-scatter.5.cloned.1.call-done = bf16[2,64,704]{2,1,0:T(8,128)(2,1)} async-done(((bf16[2,1024,704]{2,1,0:T(8,128)(2,1)}), bf16[2,64,704]{2,1,0:T(8,128)(2,1)}) %reduce-scatter.5.cloned.1.call-update) | async-done | bytes 180240 | tf_op jit(solution)/shard_map/reduce_scatter | solution.py:128
  372.2 207.0 %reduce-scatter.3.cloned.1.call-done = bf16[2,64,704]{2,1,0:T(8,128)(2,1)} async-done(((bf16[2,1024,704]{2,1,0:T(8,128)(2,1)}), bf16[2,64,704]{2,1,0:T(8,128)(2,1)}) %reduce-scatter.3.cloned.1.call-update) | async-done | bytes 180240 | tf_op jit(solution)/shard_map/reduce_scatter | solution.py:122
  (43 shorter events, 5.7 us)
Async XLA Ops:
  7.2 100.2 %copy-start = (bf16[1,2,704,1024]{3,2,1,0:T(8,128)(2,1)S(1)}, bf16[1,2,704,1024]{3,2,1,0:T(8,128)(2,1)}, u32[]{:S(2)}) copy-start(bf16[1,2,704,1024]{3,2,1,0:T(8,128)(2,1)} %param.10) | copy-start | bytes 8650756
  7.2 37.6 %copy-start.7 = (f32[1,24,6]{1,0,2:T(1,128)S(1)}, f32[1,24,6]{1,0,2:T(1,128)}, u32[]{:S(2)}) copy-start(f32[1,24,6]{1,0,2:T(1,128)} %param.8) | copy-start | bytes 1732
  7.2 37.8 %copy-start.6 = (bf16[1,24,1024]{2,1,0:T(8,128)(2,1)S(1)}, bf16[1,24,1024]{2,1,0:T(8,128)(2,1)}, u32[]{:S(2)}) copy-start(bf16[1,24,1024]{2,1,0:T(8,128)(2,1)} %param.11) | copy-start | bytes 147460
  13.6 58.0 %all-to-all-start = ((bf16[16,1,2,6,1024]{4,2,3,1,0:T(2,128)(2,1)}), bf16[16,1,2,6,1024]{4,2,3,1,0:T(2,128)(2,1)}, u32[]{:S(2)}, u32[]{:S(2)}) async-start(bf16[16,1,2,6,1024]{4,2,3,1,0:T(2,128)(2,1)} %copy.59), calls=%async_computation | async-start | bytes 786432 | tf_op jit(solution)/shard_map/all_to_all | solution.py:31
  45.0 0.6 copy-start.3
  71.6 32.1 %all-to-all-start.2 = ((bf16[16,1,2,6,1024]{4,2,3,1,0:T(2,128)(2,1)}), bf16[16,1,2,6,1024]{4,2,3,1,0:T(2,128)(2,1)}, u32[]{:S(2)}, u32[]{:S(2)}) async-start(bf16[16,1,2,6,1024]{4,2,3,1,0:T(2,128)(2,1)} %copy.65), calls=%async_computation.2 | async-start | bytes 786432 | tf_op jit(solution)/shard_map/all_to_all | solution.py:31
  78.0 294.2 %reduce-scatter.5.cloned.1.call-start = ((), (), s32[]{:S(2)}) async-start(), calls=%async_computation.7 | async-start | bytes 3342336 | tf_op jit(solution)/shard_map/reduce_scatter | solution.py:128
  81.0 26.4 %copy-start.2 = (f32[16,2,6,704]{3,0,2,1:T(8,128)}, f32[16,2,6,704]{3,0,2,1:T(8,128)S(1)}, u32[]{:S(2)}) copy-start(f32[16,2,6,704]{3,0,2,1:T(8,128)S(1)} %fusion.17) | copy-start | bytes 1622020
  109.2 40.3 %all-to-all-start.1 = ((bf16[16,1,2,6,1024]{4,2,3,1,0:T(2,128)(2,1)}), bf16[16,1,2,6,1024]{4,2,3,1,0:T(2,128)(2,1)S(1)}, u32[]{:S(2)}, u32[]{:S(2)}) async-start(bf16[16,1,2,6,1024]{4,2,3,1,0:T(2,128)(2,1)} %copy.61), calls=%async_computation.1 | async-start | bytes 786432 | tf_op jit(solution)/shard_map/all_to_all | solution.py:35
  123.9 455.3 %reduce-scatter.3.cloned.1.call-start = ((), (), s32[]{:S(2)}) async-start(), calls=%async_computation.6 | async-start | bytes 3342336 | tf_op jit(solution)/shard_map/reduce_scatter | solution.py:122
  126.2 0.7 copy-start.5
  133.2 68.5 %copy-start.4 = (f32[24,1024]{1,0:T(8,128)S(1)}, f32[24,1024]{1,0:T(8,128)}, u32[]{:S(2)}) copy-start(f32[24,1024]{1,0:T(8,128)} %copy-done.3) | copy-start | bytes 294916
  149.4 11.8 %copy-start.1 = (bf16[16,1,2,6,1024]{4,2,3,1,0:T(2,128)(2,1)}, bf16[16,1,2,6,1024]{4,2,3,1,0:T(2,128)(2,1)S(1)}, u32[]{:S(2)}) copy-start(bf16[16,1,2,6,1024]{4,2,3,1,0:T(2,128)(2,1)S(1)} %all-to-all-done.1) | copy-start | bytes 1179652
  149.4 44.2 %all-to-all-start.3 = ((bf16[16,1,2,6,1024]{4,2,3,1,0:T(2,128)(2,1)}), bf16[16,1,2,6,1024]{4,2,3,1,0:T(2,128)(2,1)}, u32[]{:S(2)}, u32[]{:S(2)}) async-start(bf16[16,1,2,6,1024]{4,2,3,1,0:T(2,128)(2,1)} %copy.67), calls=%async_computation.3 | async-start | bytes 786432 | tf_op jit(solution)/shard_map/all_to_all | solution.py:35
  196.9 7.4 %collective-permute-start = (bf16[24,1024]{1,0:T(8,128)(2,1)S(1)}, bf16[24,1024]{1,0:T(8,128)(2,1)S(1)}, u32[]{:S(2)}, u32[]{:S(2)}) collective-permute-start(bf16[24,1024]{1,0:T(8,128)(2,1)S(1)} %convolution_reduce_fusion), channel_id=1, source_target_pairs={{256,0},{512,256},{768,512},{0,768},{257,1},{513,257},{769,513},{1... | collective-permute-start | bytes 147464 | tf_op jit(solution)/shard_map/ppermute | solution.py:10
Sparse Core Ops, SparseCore 0:
  107.5 264.6 reduce-scatter.4
  376.2 202.9 reduce-scatter.2
where the time goes:
time: 588 us; the launch traced here: 587 us
  waiting for transfers between devices  464 us (79%)
  starting transfers between devices  69 us (12%)
  matrix products  21.9 us (4%)
  local copies, waits for them, and re-layouts  17.2 us (3%)
  between operations  14.3 us (2%)
    reduce_scatter x1, waiting for transfers between devices, body(): lax.psum_scatter(weight_term(arrived_inputs, hidden_grad).astype(jnp.bflo...  207 us
    reduce_scatter x1, waiting for transfers between devices, body(): lax.psum_scatter(weight_term(arrived_grads, activated).astype(jnp.bfloat1...  168 us
    all_to_all x2, waiting for transfers between devices, from_experts(): lax.all_to_all(stacked, 'expert', split_axis=0, concat_axis=0, tiled=True)  45.5 us
    all_to_all x2, waiting for transfers between devices, to_experts(): lax.all_to_all(stacked, 'expert', split_axis=0, concat_axis=0, tiled=True)  43 us
    all_to_all x2, starting transfers between devices, to_experts(): lax.all_to_all(stacked, 'expert', split_axis=0, concat_axis=0, tiled=True)  37.6 us
    all_to_all x2, starting transfers between devices, from_experts(): lax.all_to_all(stacked, 'expert', split_axis=0, concat_axis=0, tiled=True)  26.5 us
  transfers between devices with their start and end apart: 7, of which 6 were waited for; matrix products, arithmetic and copies ran while one was open for 5% of the time, Pallas kernels for 0%

commit v1 on v0

v1 whole, which is shorter than its diff:
```python
import functools

import jax
import jax.numpy as jnp
from jax import lax
from jax.experimental import pallas as pl
from jax.experimental.pallas import tpu as pltpu
from jax.sharding import PartitionSpec as P

PLANE = ("dp", "expert")
ROUND = ("section", "dp", "expert")
LANES = 128
CAPACITY = 6
F32 = jnp.float32
BF16 = jnp.bfloat16

Z_LO, Y, Z_HI, CORES = 16, 4, 2, 2
Z = Z_LO * Z_HI
CLASS = 4


def place(z, y, core):
    return (z % Z_LO) * (Y * Z_HI * CORES) + y * (Z_HI * CORES) + (z // Z_LO) * CORES + core


def moved(dz=0, dy=0, flip=0):
    return [
        (place(z, y, c), place((z + dz) % Z, (y + dy) % Y, c ^ flip))
        for z in range(Z)
        for y in range(Y)
        for c in range(CORES)
    ]


def send(block, dz=0, dy=0, flip=0):
    return lax.ppermute(block, PLANE, moved(dz, dy, flip))


def send_in_block(block, flip):
    pairs = [
        (place(z, y, c), place(z ^ flip, y, c))
        for z in range(Z)
        for y in range(Y)
        for c in range(CORES)
    ]
    return lax.ppermute(block, PLANE, pairs)


def send_to_section_before(block, sections, dz=0):
    plane = Z * Y * CORES
    pairs = [
        (s * plane + a, ((s - 1) % sections) * plane + b)
        for s in range(sections)
        for a, b in moved(dz)
    ]
    return lax.ppermute(block, ROUND, pairs)


def dot(a, b, over):
    return lax.dot_general(a, b, (over, ((), ())), preferred_element_type=F32)


NN = ((1,), (0,))
NT = ((1,), (1,))
TN = ((0,), (0,))


def experts_kernel(
    place_ref, *refs, pieces, groups, tok, feat, units, features_out, capacity
):
    piece_refs = refs[:pieces]
    up_ref, down_ref, keep_ref, send_ref, parts_out, xs, gs, us, acts, hgs, sums = refs[pieces:]
    first = place_ref[0]
    column = place_ref[1]
    spot = place_ref[2]
    per_piece = 2 * tok
    rows = pieces * per_piece
    slots = rows // tok * capacity
    wide = 2 * LANES
    lane = lax.broadcasted_iota(jnp.int32, (rows, LANES), 1)
    r_row = lax.broadcasted_iota(jnp.int32, (rows, rows), 0)
    r_col = lax.broadcasted_iota(jnp.int32, (rows, rows), 1)
    before = jnp.where((r_col <= r_row) & (r_col // tok == r_row // tok), 1.0, 0.0).astype(BF16)
    ones = jnp.ones((LANES, wide), BF16)
    base = (lax.broadcasted_iota(jnp.int32, (rows, wide), 0) // tok * capacity - 1).astype(F32)
    lane_wide = lax.broadcasted_iota(jnp.int32, (rows, wide), 1).astype(F32)
    s_lane = lax.broadcasted_iota(jnp.int32, (slots, LANES), 1)
    names = [(first + j).astype(F32) for j in range(2)]
    own = None
    own_meta = []
    for g in range(groups):
        block = jnp.concatenate(
            [r[g * per_piece : (g + 1) * per_piece, :] for r in piece_refs], axis=0
        )
        meta = block[:, 2 * feat :].astype(F32)
        at = []
        for j in range(2):
            hit = jnp.where((meta == names[j]) & (lane < 6), 1.0, 0.0).astype(BF16)
            named = dot(hit, ones, NN)
            rank = dot(before, named.astype(BF16), NN)
            target = jnp.where(named > 0.5, base + rank + j * slots, -1.0)
            at.append(target)
        picks = jnp.where((at[0] == lane_wide) & (lane_wide < slots), 1.0, 0.0) + jnp.where(
            at[1] == lane_wide, 1.0, 0.0
        )
        picks = picks.astype(BF16)
        gathered = dot(picks, block, TN)
        for j in range(2):
            part = gathered[j * slots : (j + 1) * slots]
            m = part[:, 2 * feat :]
            gates = pltpu.roll(m, LANES - 16, 1)
            match = (m == names[j]) & (s_lane < 12)
            gate = jnp.sum(jnp.where(match, gates, 0.0), axis=1, keepdims=True)
            grad = part[:, feat : 2 * feat]
            xs[j, g * slots : (g + 1) * slots, :] = part[:, :feat].astype(BF16)
            gs[j, g * slots : (g + 1) * slots, :] = (gate * grad).astype(BF16)
            if g == 0:
                us[j] = grad
                own_meta.append((match, gate))
        if g == 0:
            own = picks
    back = []
    for j in range(2):
        hidden = dot(xs[j], up_ref[j], NT)
        logistic = 1.0 / (1.0 + jnp.exp(-hidden))
        act = (hidden * logistic).astype(BF16)
        slope = logistic * (1.0 + hidden * (1.0 - logistic))
        hg = (dot(gs[j], down_ref[j], NT) * slope).astype(BF16)
        acts[...] = act
        hgs[...] = hg
        match, gate = own_meta[j]
        out = dot(acts[:slots], down_ref[j], NN).astype(BF16).astype(F32)
        dots = jnp.sum(us[j] * out, axis=1, keepdims=True)
        high = dots.astype(BF16).astype(F32)
        d = jnp.where(match, jnp.where(s_lane < 6, high, dots - high), 0.0).astype(BF16)
        rg = dot(hgs[:slots], up_ref[j], NN).astype(BF16)
        back.append(jnp.concatenate([(gate * out).astype(BF16), rg, d], axis=1))
        cols = pl.ds(pl.multiple_of(column, 256), 256)
        up_part = dot(xs[j, :, cols], hgs[...], TN).astype(BF16)
        down_part = dot(gs[j, :, cols], acts[...], TN).astype(BF16)
        sums[0] = up_part
        sums[1] = down_part
        for q in range(CLASS):
            take = pl.ds(pl.multiple_of((spot ^ q) * features_out, features_out), features_out)
            parts_out[q, 0, j] = sums[0, take, :]
            parts_out[q, 1, j] = sums[1, take, :]
    pad = jnp.zeros((wide - 2 * slots, back[0].shape[1]), BF16)
    stacked = jnp.concatenate(back + [pad], axis=0)
    result = dot(own, stacked, NN).astype(BF16)
    keep_ref[...] = result[: rows // 2]
    send_ref[...] = result[rows // 2 :]


def run_experts(pieces, up_t, down, where, tok, feat, features_out):
    units = up_t.shape[1]
    width = pieces[0].shape[1]
    groups = pieces[0].shape[0] // (2 * tok)
    rows = len(pieces) * 2 * tok
    slots = rows // tok * CAPACITY
    kernel = functools.partial(
        experts_kernel,
        pieces=len(pieces),
        groups=groups,
        tok=tok,
        feat=feat,
        units=units,
        features_out=features_out,
        capacity=CAPACITY,
    )
    vmem = pl.BlockSpec(memory_space=pltpu.VMEM)
    return pl.pallas_call(
        kernel,
        out_shape=(
            jax.ShapeDtypeStruct((rows // 2, width), BF16),
            jax.ShapeDtypeStruct((rows // 2, width), BF16),
            jax.ShapeDtypeStruct((CLASS, 2, 2, features_out, units), BF16),
        ),
        in_specs=[pl.BlockSpec(memory_space=pltpu.SMEM)] + [vmem] * (len(pieces) + 2),
        out_specs=(vmem,) * 3,
        scratch_shapes=[
            pltpu.VMEM((2, groups * slots, feat), BF16),
            pltpu.VMEM((2, groups * slots, feat), BF16),
            pltpu.VMEM((2, slots, feat), F32),
            pltpu.VMEM((groups * slots, units), BF16),
            pltpu.VMEM((groups * slots, units), BF16),
            pltpu.VMEM((2, CLASS * features_out, units), BF16),
        ],
        compiler_params=pltpu.CompilerParams(vmem_limit_bytes=56 * 1024 * 1024),
        cost_estimate=pl.CostEstimate(
            flops=8 * 10**9, bytes_accessed=16 * 10**6, transcendentals=10**6
        ),
    )(where, *pieces, up_t, down)


def body(sections, tokens, routes, gate_values, up_weight, down_weight, out_grad):
    tok, feat = tokens.shape[1:]
    top = routes.shape[2]
    gates = gate_values[0]
    names = routes[0].astype(BF16)
    high = lax.reduce_precision(gates, 8, 7)
    gap = jnp.zeros((tok, 16 - 2 * top), BF16)
    meta = jnp.concatenate(
        [names, names, gap, high.astype(BF16), (gates - high).astype(BF16)], axis=1
    )
    meta = jnp.pad(meta, ((0, 0), (0, LANES - meta.shape[1])))
    mine = jnp.concatenate([tokens[0], out_grad[0], meta], axis=1)

    across = send(mine, dz=Z_LO)
    ups, downs = [mine], [mine]
    for _ in range(3):
        ups.append(send(ups[-1], dz=CLASS))
        downs.append(send(downs[-1], dz=-CLASS))
    line = jnp.concatenate(
        [mine, across, ups[1], downs[3], ups[2], downs[2], ups[3], downs[1]], axis=0
    )
    pieces = [line] + [send(line, dy=d) for d in range(1, Y)]
    pieces = pieces + [send(p, flip=1) for p in pieces]

    z_lo = lax.axis_index("dp")
    local = up_weight.shape[1]
    features_out = feat // Z_LO
    where = jnp.stack(
        [lax.axis_index("expert") * local, z_lo // CLASS * (CLASS * features_out), z_lo % CLASS]
    ).astype(jnp.int32)
    keep, give, parts = run_experts(
        pieces, jnp.swapaxes(up_weight[0], 1, 2), down_weight[0], where, tok, feat, features_out
    )

    got = send(give, flip=1)
    both = (keep.astype(F32) + got.astype(F32)).astype(BF16).reshape(Y, 2 * tok, -1)
    total = both[0].astype(F32)
    for d in range(1, Y):
        total = total + send(both[d], dy=-d).astype(F32)
    total = total.astype(BF16)
    near, far = total[:tok], total[tok:]
    outer = jnp.concatenate([far[:, :feat], far[:, 2 * feat :]], axis=1)
    outer = send(outer, dz=Z_LO).astype(F32)
    layer_output = (near[:, :feat].astype(F32) + outer[:, :feat]).astype(BF16)
    dots = near[:, 2 * feat :].astype(F32) + outer[:, feat:]
    gate_grad = dots[:, :top] + dots[:, top : 2 * top]
    input_grad = send_to_section_before(near[:, feat : 2 * feat], sections).astype(
        F32
    ) + send_to_section_before(far[:, feat : 2 * feat], sections, dz=Z_LO).astype(F32)

    sums = parts[0].astype(F32)
    for flip in range(1, CLASS):
        sums = sums + send_in_block(parts[flip], flip).astype(F32)
    sums = sums.astype(BF16)
    return (
        layer_output[None],
        input_grad.astype(BF16)[None],
        gate_grad[None],
        sums[0][None],
        sums[1][None],
    )


def solution(mesh):
    placed = (
        P("section", ("dp", "expert"), None),
        P("section", ("dp", "expert"), None),
        P("section", ("dp", "expert"), None),
        P("section", "expert", None, None),
        P("section", "expert", None, None),
        P("section", ("dp", "expert"), None),
    )
    return jax.shard_map(
        functools.partial(body, mesh.shape["section"]),
        mesh=mesh,
        in_specs=placed,
        out_specs=(
            P("section", ("dp", "expert"), None),
            P("section", ("dp", "expert"), None),
            P("section", ("dp", "expert"), None),
            P("section", "expert", "dp", None),
            P("section", "expert", "dp", None),
        ),
        check_vma=False,
    )
```

time: 588 us -> 266 us (0.45)
  waiting for transfers between devices: 464 us -> 103 us
  starting transfers between devices: 69 us -> 132 us
  matrix products: 21.9 us -> 0 us
  Pallas kernels: 0 us -> 16.5 us
  between operations: 14.3 us -> 1.03 us
  local copies, waits for them, and re-layouts: 17.2 us -> 4.63 us
    reduce_scatter x2 -> x0, waiting for transfers between devices: 375 us -> none  [the longest x1 207 us: body(): lax.psum_scatter(weight_term(arrived_inputs, hidden_grad).astype(jnp.bflo...]
    ppermute x1 -> x24, starting transfers between devices: 4.79 us -> 132 us  [the longest x19 101 us: send(): return lax.ppermute(block, PLANE, moved(dz, dy, flip))]
    ppermute x1 -> x24, waiting for transfers between devices: 0.01 us -> 103 us  [the longest x19 70.3 us: send(): return lax.ppermute(block, PLANE, moved(dz, dy, flip))]
    all_to_all x4 -> x0, waiting for transfers between devices: 88.5 us -> none  [the longest x2 45.5 us: from_experts(): lax.all_to_all(stacked, 'expert', split_axis=0, concat_axis=0, tiled=True)]
    all_to_all x4 -> x0, starting transfers between devices: 64.1 us -> none  [the longest x2 37.6 us: to_experts(): lax.all_to_all(stacked, 'expert', split_axis=0, concat_axis=0, tiled=True)]
    dot_general x10 -> x0, matrix products: 21.9 us -> none  [the longest x2 7.43 us: weight_term(): jnp.einsum('secd,sech->edh', row_side, unit_side, preferred_element_type=...]
    pallas_call x0 -> x1, Pallas kernels: none -> 16.5 us  [run_experts(): pl.pallas_call(kernel, out_shape=(jax.ShapeDtypeStruct((rows // 2, width)...]
    another operation x7 -> x0, local copies, waits for them, and re-layouts: 6.35 us -> none  [the longest x2 2.28 us: body(): arrived_inputs = to_experts(sent_inputs[:, None])[:, 0]]
  transfers between devices with their start and end apart: 7 -> 24, of which waited for: 6 -> 13; matrix products, arithmetic and copies ran while one was open for 5% -> 2% of each run, Pallas kernels for 0% -> 0%
where the time goes in v1:
time: 266 us; the launch traced here: 262 us
  starting transfers between devices  132 us (50%)
  waiting for transfers between devices  103 us (39%)
  Pallas kernels  16.5 us (6%)
  local copies, waits for them, and re-layouts  4.63 us (2%)
  other arithmetic  4.31 us (2%)
    ppermute x19, starting transfers between devices, send(): return lax.ppermute(block, PLANE, moved(dz, dy, flip))  101 us
    ppermute x19, waiting for transfers between devices, send(): return lax.ppermute(block, PLANE, moved(dz, dy, flip))  70.3 us
    ppermute x3, waiting for transfers between devices, send_in_block(): return lax.ppermute(block, PLANE, pairs)  31.5 us
    pallas_call x1, Pallas kernels, run_experts(): pl.pallas_call(kernel, out_shape=(jax.ShapeDtypeStruct((rows // 2, width)...  16.5 us
    ppermute x2, starting transfers between devices, send_to_section_before(): return lax.ppermute(block, ROUND, pairs)  15.8 us
    ppermute x3, starting transfers between devices, send_in_block(): return lax.ppermute(block, PLANE, pairs)  14.8 us
  transfers between devices with their start and end apart: 24, of which 13 were waited for; matrix products, arithmetic and copies ran while one was open for 2% of the time, Pallas kernels for 0%

profile of v1, /device:TPU:24, one launch (start us, length us, event | category | flops | bytes accessed | tf_op | source)
XLA Modules:
  0.0 262.0 jit_solution(3264268456890466780)
XLA Ops:
  3.1 9.1 %collective-permute-start.1 = (bf16[24,2176]{1,0:T(8,128)(2,1)S(1)}, bf16[24,2176]{1,0:T(8,128)(2,1)S(1)}, u32[]{:S(2)}, u32[]{:S(2)}) collective-permute-start(bf16[24,2176]{1,0:T(8,128)(2,1)S(1)} %get-tuple-element.27), channel_id=1, source_target_pairs={{0,64},{1,65},{4,68},{5,69},{8,72},{9,73},{12,76},{13,77},{16,80},... | collective-permute-start | bytes 313352 | tf_op jit(solution)/shard_map/ppermute | solution.py:36
  12.2 12.8 %collective-permute-start.2 = (bf16[24,2176]{1,0:T(8,128)(2,1)S(1)}, bf16[24,2176]{1,0:T(8,128)(2,1)S(1)}, u32[]{:S(2)}, u32[]{:S(2)}) collective-permute-start(bf16[24,2176]{1,0:T(8,128)(2,1)S(1)} %get-tuple-element.27), channel_id=1, source_target_pairs={{0,194},{1,195},{4,198},{5,199},{8,202},{9,203},{12,206},{13,207},... | collective-permute-start | bytes 313352 | tf_op jit(solution)/shard_map/ppermute | solution.py:36
  25.1 16.8 %collective-permute-start = (bf16[24,2176]{1,0:T(8,128)(2,1)S(1)}, bf16[24,2176]{1,0:T(8,128)(2,1)S(1)}, u32[]{:S(2)}, u32[]{:S(2)}) collective-permute-start(bf16[24,2176]{1,0:T(8,128)(2,1)S(1)} %get-tuple-element.27), channel_id=1, source_target_pairs={{0,2},{1,3},{4,6},{5,7},{8,10},{9,11},{12,14},{13,15},{16,18},{17,... | collective-permute-start | bytes 313352 | tf_op jit(solution)/shard_map/ppermute | solution.py:36
  41.9 4.3 %collective-permute-start.5 = (bf16[24,2176]{1,0:T(8,128)(2,1)S(1)}, bf16[24,2176]{1,0:T(8,128)(2,1)S(1)}, u32[]{:S(2)}, u32[]{:S(2)}) collective-permute-start(bf16[24,2176]{1,0:T(8,128)(2,1)S(1)} %collective-permute-done.1), channel_id=1, source_target_pairs={{0,64},{1,65},{4,68},{5,69},{8,72},{9,73},{12,76},{13,77},{16,80},... | collective-permute-start | bytes 313352 | tf_op jit(solution)/shard_map/ppermute | solution.py:36
  46.2 5.5 %collective-permute-start.3 = (bf16[24,2176]{1,0:T(8,128)(2,1)S(1)}, bf16[24,2176]{1,0:T(8,128)(2,1)S(1)}, u32[]{:S(2)}, u32[]{:S(2)}) collective-permute-start(bf16[24,2176]{1,0:T(8,128)(2,1)S(1)} %collective-permute-done.2), channel_id=1, source_target_pairs={{0,194},{1,195},{4,198},{5,199},{8,202},{9,203},{12,206},{13,207},... | collective-permute-start | bytes 313352 | tf_op jit(solution)/shard_map/ppermute | solution.py:36
  51.7 18.2 %collective-permute-done.3 = bf16[24,2176]{1,0:T(8,128)(2,1)S(1)} collective-permute-done((bf16[24,2176]{1,0:T(8,128)(2,1)S(1)}, bf16[24,2176]{1,0:T(8,128)(2,1)S(1)}, u32[]{:S(2)}, u32[]{:S(2)}) %collective-permute-start.3) | collective-permute-done | bytes 104480 | tf_op jit(solution)/shard_map/ppermute | solution.py:36
  69.8 5.8 %collective-permute-start.4 = (bf16[24,2176]{1,0:T(8,128)(2,1)S(1)}, bf16[24,2176]{1,0:T(8,128)(2,1)S(1)}, u32[]{:S(2)}, u32[]{:S(2)}) collective-permute-start(bf16[24,2176]{1,0:T(8,128)(2,1)S(1)} %collective-permute-done.3), channel_id=1, source_target_pairs={{0,194},{1,195},{4,198},{5,199},{8,202},{9,203},{12,206},{13,207},... | collective-permute-start | bytes 313352 | tf_op jit(solution)/shard_map/ppermute | solution.py:36
  75.7 3.9 %collective-permute-start.6 = (bf16[24,2176]{1,0:T(8,128)(2,1)S(1)}, bf16[24,2176]{1,0:T(8,128)(2,1)S(1)}, u32[]{:S(2)}, u32[]{:S(2)}) collective-permute-start(bf16[24,2176]{1,0:T(8,128)(2,1)S(1)} %collective-permute-done.5), channel_id=1, source_target_pairs={{0,64},{1,65},{4,68},{5,69},{8,72},{9,73},{12,76},{13,77},{16,80},... | collective-permute-start | bytes 313352 | tf_op jit(solution)/shard_map/ppermute | solution.py:36
  79.6 2.7 %collective-permute-done.4 = bf16[24,2176]{1,0:T(8,128)(2,1)S(1)} collective-permute-done((bf16[24,2176]{1,0:T(8,128)(2,1)S(1)}, bf16[24,2176]{1,0:T(8,128)(2,1)S(1)}, u32[]{:S(2)}, u32[]{:S(2)}) %collective-permute-start.4) | collective-permute-done | bytes 104480 | tf_op jit(solution)/shard_map/ppermute | solution.py:36
  82.4 3.8 %collective-permute-done.6 = bf16[24,2176]{1,0:T(8,128)(2,1)S(1)} collective-permute-done((bf16[24,2176]{1,0:T(8,128)(2,1)S(1)}, bf16[24,2176]{1,0:T(8,128)(2,1)S(1)}, u32[]{:S(2)}, u32[]{:S(2)}) %collective-permute-start.6) | collective-permute-done | bytes 104480 | tf_op jit(solution)/shard_map/ppermute | solution.py:36
  86.3 2.7 %collective-permute-start.9 = (bf16[192,2176]{1,0:T(8,128)(2,1)S(1)}, bf16[192,2176]{1,0:T(8,128)(2,1)S(1)}, u32[]{:S(2)}, u32[]{:S(2)}) collective-permute-start(bf16[192,2176]{1,0:T(8,128)(2,1)S(1)} %constant_dynamic-update-slice_fusion.refs_0_), channel_id=1, source_target_pairs={{0,12},{1,13},{4,0},{5,1},{8,4},{9,5},{12,8},{13,9},{16,28},{17,29... | collective-permute-start | bytes 2506760 | tf_op jit(solution)/shard_map/ppermute | solution.py:36
  88.9 6.0 %collective-permute-start.8 = (bf16[192,2176]{1,0:T(8,128)(2,1)S(1)}, bf16[192,2176]{1,0:T(8,128)(2,1)S(1)}, u32[]{:S(2)}, u32[]{:S(2)}) collective-permute-start(bf16[192,2176]{1,0:T(8,128)(2,1)S(1)} %constant_dynamic-update-slice_fusion.refs_0_), channel_id=1, source_target_pairs={{0,8},{1,9},{4,12},{5,13},{8,0},{9,1},{12,4},{13,5},{16,24},{17,25... | collective-permute-start | bytes 2506760 | tf_op jit(solution)/shard_map/ppermute | solution.py:36
  95.0 1.9 collective-permute-start.7
  96.9 1.9 collective-permute-start.10
  98.8 12.5 %collective-permute-done.9.refs_3_ = bf16[192,2176]{1,0:T(8,128)(2,1)S(1)} collective-permute-done((bf16[192,2176]{1,0:T(8,128)(2,1)S(1)}, bf16[192,2176]{1,0:T(8,128)(2,1)S(1)}, u32[]{:S(2)}, u32[]{:S(2)}) %collective-permute-start.9) | collective-permute-done | bytes 835616 | tf_op jit(solution)/shard_map/ppermute | solution.py:36
  113.3 13.5 %collective-permute-done.8.refs_2_ = bf16[192,2176]{1,0:T(8,128)(2,1)S(1)} collective-permute-done((bf16[192,2176]{1,0:T(8,128)(2,1)S(1)}, bf16[192,2176]{1,0:T(8,128)(2,1)S(1)}, u32[]{:S(2)}, u32[]{:S(2)}) %collective-permute-start.8) | collective-permute-done | bytes 835616 | tf_op jit(solution)/shard_map/ppermute | solution.py:36
  128.8 2.4 collective-permute-start.11
  133.3 16.5 %shard_map.101 = (bf16[192,2176]{1,0:T(8,128)(2,1)}, bf16[192,2176]{1,0:T(8,128)(2,1)}, bf16[4,2,2,64,704]{4,3,2,1,0:T(8,128)(2,1)}) custom-call(s32[3]{0:T(128)} %pad_add_fusion.place_ref, bf16[192,2176]{1,0:T(8,128)(2,1)} %copy-done.1, bf16[192,2176]{1,0:T(8,128)(2,1)} %copy-done.4, bf16[192,2176]{1,0:T(8,128)(2,1)} %copy-done.3, ...), custom_call_target="tpu_custom_call" | custom-call | flops 8000000000 | bytes 16000000 | tf_op jit(solution)/shard_map/pallas_call | solution.py:171
  149.7 2.3 collective-permute-start.14
  153.4 1.9 collective-permute-start.21
  155.3 11.0 %collective-permute-start.23 = (bf16[2,2,64,704]{3,2,1,0:T(8,128)(2,1)S(1)}, bf16[2,2,64,704]{3,2,1,0:T(8,128)(2,1)S(1)}, u32[]{:S(2)}, u32[]{:S(2)}) collective-permute-start(bf16[2,2,64,704]{3,2,1,0:T(8,128)(2,1)S(1)} %get-tuple-element.17), channel_id=1, source_target_pairs={{0,48},{1,49},{4,52},{5,53},{8,56},{9,57},{12,60},{13,61},{16,32},... | collective-permute-start | bytes 1081352 | tf_op jit(solution)/shard_map/ppermute | solution.py:46
  166.3 1.9 collective-permute-start.22
  168.3 14.6 %collective-permute-done.23 = bf16[2,2,64,704]{3,2,1,0:T(8,128)(2,1)S(1)} collective-permute-done((bf16[2,2,64,704]{3,2,1,0:T(8,128)(2,1)S(1)}, bf16[2,2,64,704]{3,2,1,0:T(8,128)(2,1)S(1)}, u32[]{:S(2)}, u32[]{:S(2)}) %collective-permute-start.23) | collective-permute-done | bytes 360480 | tf_op jit(solution)/shard_map/ppermute | solution.py:46
  182.8 17.0 %collective-permute-done.22 = bf16[2,2,64,704]{3,2,1,0:T(8,128)(2,1)S(1)} collective-permute-done((bf16[2,2,64,704]{3,2,1,0:T(8,128)(2,1)S(1)}, bf16[2,2,64,704]{3,2,1,0:T(8,128)(2,1)S(1)}, u32[]{:S(2)}, u32[]{:S(2)}) %collective-permute-start.22) | collective-permute-done | bytes 360480 | tf_op jit(solution)/shard_map/ppermute | solution.py:46
  201.3 1.9 collective-permute-start.15
  203.2 5.1 %collective-permute-start.17 = (bf16[48,2176]{1,0:T(8,128)(2,1)S(1)}, bf16[48,2176]{1,0:T(8,128)(2,1)S(1)}, u32[]{:S(2)}, u32[]{:S(2)}) collective-permute-start(bf16[48,2176]{1,0:T(8,128)(2,1)S(1)} %get-tuple-element.20), channel_id=1, source_target_pairs={{0,4},{1,5},{4,8},{5,9},{8,12},{9,13},{12,0},{13,1},{16,20},{17,21... | collective-permute-start | bytes 626696 | tf_op jit(solution)/shard_map/ppermute | solution.py:36
  208.3 1.9 collective-permute-start.16
  211.3 5.7 %collective-permute-done.17 = bf16[48,2176]{1,0:T(8,128)(2,1)S(1)} collective-permute-done((bf16[48,2176]{1,0:T(8,128)(2,1)S(1)}, bf16[48,2176]{1,0:T(8,128)(2,1)S(1)}, u32[]{:S(2)}, u32[]{:S(2)}) %collective-permute-start.17) | collective-permute-done | bytes 208928 | tf_op jit(solution)/shard_map/ppermute | solution.py:36
  218.2 4.7 %collective-permute-start.19 = (bf16[24,1024]{1,0:T(8,128)(2,1)S(1)}, bf16[24,1024]{1,0:T(8,128)(2,1)S(1)}, u32[]{:S(2)}, u32[]{:S(2)}) collective-permute-start(bf16[24,1024]{1,0:T(8,128)(2,1)S(1)} %get-tuple-element.24), channel_id=1, source_target_pairs={{0,768},{1,769},{4,772},{5,773},{8,776},{9,777},{12,780},{13,781},... | collective-permute-start | bytes 147464 | tf_op jit(solution)/shard_map/ppermute | solution.py:56
  222.9 11.2 %collective-permute-start.20 = (bf16[24,1024]{1,0:T(8,128)(2,1)S(1)}, bf16[24,1024]{1,0:T(8,128)(2,1)S(1)}, u32[]{:S(2)}, u32[]{:S(2)}) collective-permute-start(bf16[24,1024]{1,0:T(8,128)(2,1)S(1)} %get-tuple-element.25), channel_id=1, source_target_pairs={{0,770},{1,771},{4,774},{5,775},{8,778},{9,779},{12,782},{13,783},... | collective-permute-start | bytes 147464 | tf_op jit(solution)/shard_map/ppermute | solution.py:56
  234.1 13.2 %collective-permute-start.18 = (bf16[24,1152]{1,0:T(8,128)(2,1)S(1)}, bf16[24,1152]{1,0:T(8,128)(2,1)S(1)}, u32[]{:S(2)}, u32[]{:S(2)}) collective-permute-start(bf16[24,1152]{1,0:T(8,128)(2,1)S(1)} %pad_maximum_fusion), channel_id=1, source_target_pairs={{0,2},{1,3},{4,6},{5,7},{8,10},{9,11},{12,14},{13,15},{16,18},{17,... | collective-permute-start | bytes 165896 | tf_op jit(solution)/shard_map/ppermute | solution.py:36
  249.7 11.0 %collective-permute-done.18 = bf16[24,1152]{1,0:T(8,128)(2,1)S(1)} collective-permute-done((bf16[24,1152]{1,0:T(8,128)(2,1)S(1)}, bf16[24,1152]{1,0:T(8,128)(2,1)S(1)}, u32[]{:S(2)}, u32[]{:S(2)}) %collective-permute-start.18) | collective-permute-done | bytes 55328 | tf_op jit(solution)/shard_map/ppermute | solution.py:36
  (57 shorter events, 17.3 us)
Async XLA Ops:
  3.1 38.7 %collective-permute-start.1 = (bf16[24,2176]{1,0:T(8,128)(2,1)S(1)}, bf16[24,2176]{1,0:T(8,128)(2,1)S(1)}, u32[]{:S(2)}, u32[]{:S(2)}) collective-permute-start(bf16[24,2176]{1,0:T(8,128)(2,1)S(1)} %get-tuple-element.27), channel_id=1, source_target_pairs={{0,64},{1,65},{4,68},{5,69},{8,72},{9,73},{12,76},{13,77},{16,80},... | collective-permute-start | bytes 313352 | tf_op jit(solution)/shard_map/ppermute | solution.py:36
  12.2 34.0 %collective-permute-start.2 = (bf16[24,2176]{1,0:T(8,128)(2,1)S(1)}, bf16[24,2176]{1,0:T(8,128)(2,1)S(1)}, u32[]{:S(2)}, u32[]{:S(2)}) collective-permute-start(bf16[24,2176]{1,0:T(8,128)(2,1)S(1)} %get-tuple-element.27), channel_id=1, source_target_pairs={{0,194},{1,195},{4,198},{5,199},{8,202},{9,203},{12,206},{13,207},... | collective-permute-start | bytes 313352 | tf_op jit(solution)/shard_map/ppermute | solution.py:36
  25.1 26.6 %collective-permute-start = (bf16[24,2176]{1,0:T(8,128)(2,1)S(1)}, bf16[24,2176]{1,0:T(8,128)(2,1)S(1)}, u32[]{:S(2)}, u32[]{:S(2)}) collective-permute-start(bf16[24,2176]{1,0:T(8,128)(2,1)S(1)} %get-tuple-element.27), channel_id=1, source_target_pairs={{0,2},{1,3},{4,6},{5,7},{8,10},{9,11},{12,14},{13,15},{16,18},{17,... | collective-permute-start | bytes 313352 | tf_op jit(solution)/shard_map/ppermute | solution.py:36
  41.9 33.8 %collective-permute-start.5 = (bf16[24,2176]{1,0:T(8,128)(2,1)S(1)}, bf16[24,2176]{1,0:T(8,128)(2,1)S(1)}, u32[]{:S(2)}, u32[]{:S(2)}) collective-permute-start(bf16[24,2176]{1,0:T(8,128)(2,1)S(1)} %collective-permute-done.1), channel_id=1, source_target_pairs={{0,64},{1,65},{4,68},{5,69},{8,72},{9,73},{12,76},{13,77},{16,80},... | collective-permute-start | bytes 313352 | tf_op jit(solution)/shard_map/ppermute | solution.py:36
  46.2 23.7 %collective-permute-start.3 = (bf16[24,2176]{1,0:T(8,128)(2,1)S(1)}, bf16[24,2176]{1,0:T(8,128)(2,1)S(1)}, u32[]{:S(2)}, u32[]{:S(2)}) collective-permute-start(bf16[24,2176]{1,0:T(8,128)(2,1)S(1)} %collective-permute-done.2), channel_id=1, source_target_pairs={{0,194},{1,195},{4,198},{5,199},{8,202},{9,203},{12,206},{13,207},... | collective-permute-start | bytes 313352 | tf_op jit(solution)/shard_map/ppermute | solution.py:36
  69.8 12.5 %collective-permute-start.4 = (bf16[24,2176]{1,0:T(8,128)(2,1)S(1)}, bf16[24,2176]{1,0:T(8,128)(2,1)S(1)}, u32[]{:S(2)}, u32[]{:S(2)}) collective-permute-start(bf16[24,2176]{1,0:T(8,128)(2,1)S(1)} %collective-permute-done.3), channel_id=1, source_target_pairs={{0,194},{1,195},{4,198},{5,199},{8,202},{9,203},{12,206},{13,207},... | collective-permute-start | bytes 313352 | tf_op jit(solution)/shard_map/ppermute | solution.py:36
  75.7 10.5 %collective-permute-start.6 = (bf16[24,2176]{1,0:T(8,128)(2,1)S(1)}, bf16[24,2176]{1,0:T(8,128)(2,1)S(1)}, u32[]{:S(2)}, u32[]{:S(2)}) collective-permute-start(bf16[24,2176]{1,0:T(8,128)(2,1)S(1)} %collective-permute-done.5), channel_id=1, source_target_pairs={{0,64},{1,65},{4,68},{5,69},{8,72},{9,73},{12,76},{13,77},{16,80},... | collective-permute-start | bytes 313352 | tf_op jit(solution)/shard_map/ppermute | solution.py:36
  86.3 47.0 %copy-start.1 = (bf16[192,2176]{1,0:T(8,128)(2,1)}, bf16[192,2176]{1,0:T(8,128)(2,1)S(1)}, u32[]{:S(2)}) copy-start(bf16[192,2176]{1,0:T(8,128)(2,1)S(1)} %constant_dynamic-update-slice_fusion.refs_0_) | copy-start | bytes 2506756
  86.3 25.1 %collective-permute-start.9 = (bf16[192,2176]{1,0:T(8,128)(2,1)S(1)}, bf16[192,2176]{1,0:T(8,128)(2,1)S(1)}, u32[]{:S(2)}, u32[]{:S(2)}) collective-permute-start(bf16[192,2176]{1,0:T(8,128)(2,1)S(1)} %constant_dynamic-update-slice_fusion.refs_0_), channel_id=1, source_target_pairs={{0,12},{1,13},{4,0},{5,1},{8,4},{9,5},{12,8},{13,9},{16,28},{17,29... | collective-permute-start | bytes 2506760 | tf_op jit(solution)/shard_map/ppermute | solution.py:36
  88.9 37.9 %collective-permute-start.8 = (bf16[192,2176]{1,0:T(8,128)(2,1)S(1)}, bf16[192,2176]{1,0:T(8,128)(2,1)S(1)}, u32[]{:S(2)}, u32[]{:S(2)}) collective-permute-start(bf16[192,2176]{1,0:T(8,128)(2,1)S(1)} %constant_dynamic-update-slice_fusion.refs_0_), channel_id=1, source_target_pairs={{0,8},{1,9},{4,12},{5,13},{8,0},{9,1},{12,4},{13,5},{16,24},{17,25... | collective-permute-start | bytes 2506760 | tf_op jit(solution)/shard_map/ppermute | solution.py:36
  95.0 33.8 %collective-permute-start.7 = (bf16[192,2176]{1,0:T(8,128)(2,1)S(1)}, bf16[192,2176]{1,0:T(8,128)(2,1)S(1)}, u32[]{:S(2)}, u32[]{:S(2)}) collective-permute-start(bf16[192,2176]{1,0:T(8,128)(2,1)S(1)} %constant_dynamic-update-slice_fusion.refs_0_), channel_id=1, source_target_pairs={{0,4},{1,5},{4,8},{5,9},{8,12},{9,13},{12,0},{13,1},{16,20},{17,21... | collective-permute-start | bytes 2506760 | tf_op jit(solution)/shard_map/ppermute | solution.py:36
  96.9 34.9 %collective-permute-start.10 = (bf16[192,2176]{1,0:T(8,128)(2,1)S(1)}, bf16[192,2176]{1,0:T(8,128)(2,1)}, u32[]{:S(2)}, u32[]{:S(2)}) collective-permute-start(bf16[192,2176]{1,0:T(8,128)(2,1)S(1)} %constant_dynamic-update-slice_fusion.refs_0_), channel_id=1, source_target_pairs={{0,1},{1,0},{4,5},{5,4},{8,9},{9,8},{12,13},{13,12},{16,17},{17,16... | collective-permute-start | bytes 2506760 | tf_op jit(solution)/shard_map/ppermute | solution.py:36
  111.4 21.9 %copy-start.2 = (bf16[192,2176]{1,0:T(8,128)(2,1)}, bf16[192,2176]{1,0:T(8,128)(2,1)S(1)}, u32[]{:S(2)}) copy-start(bf16[192,2176]{1,0:T(8,128)(2,1)S(1)} %collective-permute-done.9.refs_3_) | copy-start | bytes 2506756
  111.4 20.4 %collective-permute-start.13 = (bf16[192,2176]{1,0:T(8,128)(2,1)S(1)}, bf16[192,2176]{1,0:T(8,128)(2,1)}, u32[]{:S(2)}, u32[]{:S(2)}) collective-permute-start(bf16[192,2176]{1,0:T(8,128)(2,1)S(1)} %collective-permute-done.9.refs_3_), channel_id=1, source_target_pairs={{0,1},{1,0},{4,5},{5,4},{8,9},{9,8},{12,13},{13,12},{16,17},{17,16... | collective-permute-start | bytes 2506760 | tf_op jit(solution)/shard_map/ppermute | solution.py:36
  126.8 6.5 %copy-start.3 = (bf16[192,2176]{1,0:T(8,128)(2,1)}, bf16[192,2176]{1,0:T(8,128)(2,1)S(1)}, u32[]{:S(2)}) copy-start(bf16[192,2176]{1,0:T(8,128)(2,1)S(1)} %collective-permute-done.8.refs_2_) | copy-start | bytes 2506756
  126.8 5.0 %collective-permute-start.12 = (bf16[192,2176]{1,0:T(8,128)(2,1)S(1)}, bf16[192,2176]{1,0:T(8,128)(2,1)}, u32[]{:S(2)}, u32[]{:S(2)}) collective-permute-start(bf16[192,2176]{1,0:T(8,128)(2,1)S(1)} %collective-permute-done.8.refs_2_), channel_id=1, source_target_pairs={{0,1},{1,0},{4,5},{5,4},{8,9},{9,8},{12,13},{13,12},{16,17},{17,16... | collective-permute-start | bytes 2506760 | tf_op jit(solution)/shard_map/ppermute | solution.py:36
  128.8 4.5 %copy-start.4 = (bf16[192,2176]{1,0:T(8,128)(2,1)}, bf16[192,2176]{1,0:T(8,128)(2,1)S(1)}, u32[]{:S(2)}) copy-start(bf16[192,2176]{1,0:T(8,128)(2,1)S(1)} %collective-permute-done.7.refs_1_) | copy-start | bytes 2506756
  128.8 4.5 %collective-permute-start.11 = (bf16[192,2176]{1,0:T(8,128)(2,1)S(1)}, bf16[192,2176]{1,0:T(8,128)(2,1)}, u32[]{:S(2)}, u32[]{:S(2)}) collective-permute-start(bf16[192,2176]{1,0:T(8,128)(2,1)S(1)} %collective-permute-done.7.refs_1_), channel_id=1, source_target_pairs={{0,1},{1,0},{4,5},{5,4},{8,9},{9,8},{12,13},{13,12},{16,17},{17,16... | collective-permute-start | bytes 2506760 | tf_op jit(solution)/shard_map/ppermute | solution.py:36
  149.7 51.3 %collective-permute-start.14 = (bf16[192,2176]{1,0:T(8,128)(2,1)}, bf16[192,2176]{1,0:T(8,128)(2,1)S(1)}, u32[]{:S(2)}, u32[]{:S(2)}) collective-permute-start(bf16[192,2176]{1,0:T(8,128)(2,1)} %get-tuple-element.9), channel_id=1, source_target_pairs={{0,1},{1,0},{4,5},{5,4},{8,9},{9,8},{12,13},{13,12},{16,17},{17,16... | collective-permute-start | bytes 2506760 | tf_op jit(solution)/shard_map/ppermute | solution.py:36
  152.0 49.0 %copy-start = (bf16[192,2176]{1,0:T(8,128)(2,1)S(1)}, bf16[192,2176]{1,0:T(8,128)(2,1)}, u32[]{:S(2)}) copy-start(bf16[192,2176]{1,0:T(8,128)(2,1)} %get-tuple-element.8) | copy-start | bytes 2506756
  153.4 14.9 %collective-permute-start.21 = (bf16[2,2,64,704]{3,2,1,0:T(8,128)(2,1)S(1)}, bf16[2,2,64,704]{3,2,1,0:T(8,128)(2,1)S(1)}, u32[]{:S(2)}, u32[]{:S(2)}) collective-permute-start(bf16[2,2,64,704]{3,2,1,0:T(8,128)(2,1)S(1)} %get-tuple-element.16), channel_id=1, source_target_pairs={{0,16},{1,17},{4,20},{5,21},{8,24},{9,25},{12,28},{13,29},{16,0},{... | collective-permute-start | bytes 1081352 | tf_op jit(solution)/shard_map/ppermute | solution.py:46
  155.3 27.5 %collective-permute-start.23 = (bf16[2,2,64,704]{3,2,1,0:T(8,128)(2,1)S(1)}, bf16[2,2,64,704]{3,2,1,0:T(8,128)(2,1)S(1)}, u32[]{:S(2)}, u32[]{:S(2)}) collective-permute-start(bf16[2,2,64,704]{3,2,1,0:T(8,128)(2,1)S(1)} %get-tuple-element.17), channel_id=1, source_target_pairs={{0,48},{1,49},{4,52},{5,53},{8,56},{9,57},{12,60},{13,61},{16,32},... | collective-permute-start | bytes 1081352 | tf_op jit(solution)/shard_map/ppermute | solution.py:46
  166.3 33.5 %collective-permute-start.22 = (bf16[2,2,64,704]{3,2,1,0:T(8,128)(2,1)S(1)}, bf16[2,2,64,704]{3,2,1,0:T(8,128)(2,1)S(1)}, u32[]{:S(2)}, u32[]{:S(2)}) collective-permute-start(bf16[2,2,64,704]{3,2,1,0:T(8,128)(2,1)S(1)} %get-tuple-element.18), channel_id=1, source_target_pairs={{0,32},{1,33},{4,36},{5,37},{8,40},{9,41},{12,44},{13,45},{16,48},... | collective-permute-start | bytes 1081352 | tf_op jit(solution)/shard_map/ppermute | solution.py:46
  201.3 10.0 %collective-permute-start.15 = (bf16[48,2176]{1,0:T(8,128)(2,1)S(1)}, bf16[48,2176]{1,0:T(8,128)(2,1)S(1)}, u32[]{:S(2)}, u32[]{:S(2)}) collective-permute-start(bf16[48,2176]{1,0:T(8,128)(2,1)S(1)} %get-tuple-element.19), channel_id=1, source_target_pairs={{0,12},{1,13},{4,0},{5,1},{8,4},{9,5},{12,8},{13,9},{16,28},{17,29... | collective-permute-start | bytes 626696 | tf_op jit(solution)/shard_map/ppermute | solution.py:36
  203.2 13.7 %collective-permute-start.17 = (bf16[48,2176]{1,0:T(8,128)(2,1)S(1)}, bf16[48,2176]{1,0:T(8,128)(2,1)S(1)}, u32[]{:S(2)}, u32[]{:S(2)}) collective-permute-start(bf16[48,2176]{1,0:T(8,128)(2,1)S(1)} %get-tuple-element.20), channel_id=1, source_target_pairs={{0,4},{1,5},{4,8},{5,9},{8,12},{9,13},{12,0},{13,1},{16,20},{17,21... | collective-permute-start | bytes 626696 | tf_op jit(solution)/shard_map/ppermute | solution.py:36
  208.3 9.7 %collective-permute-start.16 = (bf16[48,2176]{1,0:T(8,128)(2,1)S(1)}, bf16[48,2176]{1,0:T(8,128)(2,1)S(1)}, u32[]{:S(2)}, u32[]{:S(2)}) collective-permute-start(bf16[48,2176]{1,0:T(8,128)(2,1)S(1)} %get-tuple-element.21), channel_id=1, source_target_pairs={{0,8},{1,9},{4,12},{5,13},{8,0},{9,1},{12,4},{13,5},{16,24},{17,25... | collective-permute-start | bytes 626696 | tf_op jit(solution)/shard_map/ppermute | solution.py:36
  218.2 29.1 %collective-permute-start.19 = (bf16[24,1024]{1,0:T(8,128)(2,1)S(1)}, bf16[24,1024]{1,0:T(8,128)(2,1)S(1)}, u32[]{:S(2)}, u32[]{:S(2)}) collective-permute-start(bf16[24,1024]{1,0:T(8,128)(2,1)S(1)} %get-tuple-element.24), channel_id=1, source_target_pairs={{0,768},{1,769},{4,772},{5,773},{8,776},{9,777},{12,780},{13,781},... | collective-permute-start | bytes 147464 | tf_op jit(solution)/shard_map/ppermute | solution.py:56
  222.9 26.1 %collective-permute-start.20 = (bf16[24,1024]{1,0:T(8,128)(2,1)S(1)}, bf16[24,1024]{1,0:T(8,128)(2,1)S(1)}, u32[]{:S(2)}, u32[]{:S(2)}) collective-permute-start(bf16[24,1024]{1,0:T(8,128)(2,1)S(1)} %get-tuple-element.25), channel_id=1, source_target_pairs={{0,770},{1,771},{4,774},{5,775},{8,778},{9,779},{12,782},{13,783},... | collective-permute-start | bytes 147464 | tf_op jit(solution)/shard_map/ppermute | solution.py:56
  234.1 26.5 %collective-permute-start.18 = (bf16[24,1152]{1,0:T(8,128)(2,1)S(1)}, bf16[24,1152]{1,0:T(8,128)(2,1)S(1)}, u32[]{:S(2)}, u32[]{:S(2)}) collective-permute-start(bf16[24,1152]{1,0:T(8,128)(2,1)S(1)} %pad_maximum_fusion), channel_id=1, source_target_pairs={{0,2},{1,3},{4,6},{5,7},{8,10},{9,11},{12,14},{13,15},{16,18},{17,... | collective-permute-start | bytes 165896 | tf_op jit(solution)/shard_map/ppermute | solution.py:36

commit v2 on v1

v2 whole, which is shorter than its diff:
```python
import functools

import jax
import jax.numpy as jnp
from jax import lax
from jax.experimental import pallas as pl
from jax.experimental.pallas import tpu as pltpu
from jax.sharding import PartitionSpec as P

PLANE = ("dp", "expert")
ROUND = ("section", "dp", "expert")
LANES = 128
CAPACITY = 6
F32 = jnp.float32
BF16 = jnp.bfloat16

Z_LO, Y, Z_HI, CORES = 16, 4, 2, 2
Z = Z_LO * Z_HI
CLASS = 4


def place(z, y, core):
    return (z % Z_LO) * (Y * Z_HI * CORES) + y * (Z_HI * CORES) + (z // Z_LO) * CORES + core


def moved(dz=0, dy=0, flip=0):
    return [
        (place(z, y, c), place((z + dz) % Z, (y + dy) % Y, c ^ flip))
        for z in range(Z)
        for y in range(Y)
        for c in range(CORES)
    ]


def send(block, dz=0, dy=0, flip=0):
    return lax.ppermute(block, PLANE, moved(dz, dy, flip))


LINES = [(y, c) for y in range(Y) for c in range(CORES)]
Z_CLASSES = [
    [place(z, y, c) for z in range(r, Z, CLASS)] for r in range(CLASS) for y, c in LINES
]
Z_BLOCKS = [
    [place(z + q, y, c) for q in range(CLASS)] for z in range(0, Z, CLASS) for y, c in LINES
]
Y_RINGS = [[place(z, y, c) for y in range(Y)] for z in range(Z) for c in range(CORES)]


def gather(block, rings):
    return lax.all_gather(block, PLANE, axis=0, tiled=True, axis_index_groups=rings)


def scatter_sum(block, rings):
    return lax.psum_scatter(
        block, PLANE, scatter_dimension=0, tiled=True, axis_index_groups=rings
    )


def send_to_section_before(block, sections, dz=0):
    plane = Z * Y * CORES
    pairs = [
        (s * plane + a, ((s - 1) % sections) * plane + b)
        for s in range(sections)
        for a, b in moved(dz)
    ]
    return lax.ppermute(block, ROUND, pairs)


def dot(a, b, over):
    return lax.dot_general(a, b, (over, ((), ())), preferred_element_type=F32)


NN = ((1,), (0,))
NT = ((1,), (1,))
TN = ((0,), (0,))


def experts_kernel(
    place_ref, near_ref, over_ref, up_hbm, down_hbm, keep_ref, send_ref, parts_out,
    up_ref, down_ref, xs, gs, us, picked, metas, acts, hgs, arrived, *, groups, tok, feat, capacity
):
    first = place_ref[0]
    block_at = place_ref[1]
    up_copy = pltpu.make_async_copy(up_hbm, up_ref, arrived.at[0])
    down_copy = pltpu.make_async_copy(down_hbm, down_ref, arrived.at[1])
    up_copy.start()
    down_copy.start()
    line = 2 * groups * tok
    rows = CORES * Y * 2 * tok
    slots = rows // tok * capacity
    wide = 2 * LANES
    lane = lax.broadcasted_iota(jnp.int32, (rows, LANES), 1)
    r_row = lax.broadcasted_iota(jnp.int32, (rows, rows), 0)
    r_col = lax.broadcasted_iota(jnp.int32, (rows, rows), 1)
    before = jnp.where((r_col <= r_row) & (r_col // tok == r_row // tok), 1.0, 0.0).astype(BF16)
    ones = jnp.ones((LANES, wide), BF16)
    base = (lax.broadcasted_iota(jnp.int32, (rows, wide), 0) // tok * capacity - 1).astype(F32)
    lane_wide = lax.broadcasted_iota(jnp.int32, (rows, wide), 1).astype(F32)
    s_lane = lax.broadcasted_iota(jnp.int32, (slots, LANES), 1)
    names = [(first + j).astype(F32) for j in range(2)]
    for g in range(groups):
        block = jnp.concatenate(
            [
                ref[start : start + tok, :]
                for ref in (near_ref, over_ref)
                for y in range(Y)
                for start in (y * line + g * tok, y * line + (g + groups) * tok)
            ],
            axis=0,
        )
        meta = block[:, 2 * feat :].astype(F32)
        at = []
        for j in range(2):
            hit = jnp.where((meta == names[j]) & (lane < 6), 1.0, 0.0).astype(BF16)
            named = dot(hit, ones, NN)
            rank = dot(before, named.astype(BF16), NN)
            at.append(jnp.where(named > 0.5, base + rank + j * slots, -1.0))
        picks = jnp.where((at[0] == lane_wide) & (lane_wide < slots), 1.0, 0.0) + jnp.where(
            at[1] == lane_wide, 1.0, 0.0
        )
        picks = picks.astype(BF16)
        picked[g] = picks
        gathered = dot(picks, block, TN)
        for j in range(2):
            here = slice(g * slots, (g + 1) * slots)
            part = gathered[j * slots : (j + 1) * slots]
            m = part[:, 2 * feat :]
            gates = pltpu.roll(m, LANES - 16, 1)
            match = (m == names[j]) & (s_lane < 12)
            gate = jnp.sum(jnp.where(match, gates, 0.0), axis=1, keepdims=True)
            grad = part[:, feat : 2 * feat]
            xs[j, here, :] = part[:, :feat].astype(BF16)
            us[j, here, :] = grad.astype(BF16)
            gs[j, here, :] = (gate * grad).astype(BF16)
            metas[j, here, :] = jnp.where(match, gate, 0.0)
    own = pl.ds(pl.multiple_of(block_at * slots, slots), slots)
    columns = feat // groups
    cols = pl.ds(pl.multiple_of(block_at * columns, columns), columns)
    each = columns // CLASS
    up_copy.wait()
    down_copy.wait()
    back = []
    for j in range(2):
        hidden = dot(xs[j], up_ref[j], NT)
        logistic = 1.0 / (1.0 + jnp.exp(-hidden))
        act = (hidden * logistic).astype(BF16)
        slope = logistic * (1.0 + hidden * (1.0 - logistic))
        hg = (dot(gs[j], down_ref[j], NT) * slope).astype(BF16)
        acts[...] = act
        hgs[...] = hg
        kept = metas[j, own, :]
        gate = jnp.max(kept, axis=1, keepdims=True)
        out = dot(acts[own, :], down_ref[j], NN).astype(BF16).astype(F32)
        dots = jnp.sum(us[j, own, :].astype(F32) * out, axis=1, keepdims=True)
        high = dots.astype(BF16).astype(F32)
        d = jnp.where(kept > 0.0, jnp.where(s_lane < 6, high, dots - high), 0.0).astype(BF16)
        rg = dot(hgs[own, :], up_ref[j], NN).astype(BF16)
        back.append(jnp.concatenate([(gate * out).astype(BF16), rg, d], axis=1))
        up_part = dot(xs[j, :, cols], hgs[...], TN).astype(BF16)
        down_part = dot(gs[j, :, cols], acts[...], TN).astype(BF16)
        for q in range(CLASS):
            parts_out[q, 0, j] = up_part[q * each : (q + 1) * each]
            parts_out[q, 1, j] = down_part[q * each : (q + 1) * each]
    pad = jnp.zeros((wide - 2 * slots, back[0].shape[1]), BF16)
    stacked = jnp.concatenate(back + [pad], axis=0)
    result = dot(picked[block_at], stacked, NN).astype(BF16)
    keep_ref[...] = result[: rows // 2]
    send_ref[...] = result[rows // 2 :]


def run_experts(near, over, up_t, down, where, tok, feat):
    units = up_t.shape[1]
    width = near.shape[1]
    groups = near.shape[0] // (Y * 2 * tok)
    rows = CORES * Y * 2 * tok
    slots = rows // tok * CAPACITY
    kernel = functools.partial(
        experts_kernel, groups=groups, tok=tok, feat=feat, capacity=CAPACITY
    )
    vmem = pl.BlockSpec(memory_space=pltpu.VMEM)
    anywhere = pl.BlockSpec(memory_space=pl.ANY)
    return pl.pallas_call(
        kernel,
        out_shape=(
            jax.ShapeDtypeStruct((rows // 2, width), BF16),
            jax.ShapeDtypeStruct((rows // 2, width), BF16),
            jax.ShapeDtypeStruct((CLASS, 2, 2, feat // Z_LO, units), BF16),
        ),
        in_specs=[pl.BlockSpec(memory_space=pltpu.SMEM), vmem, vmem, anywhere, anywhere],
        out_specs=(vmem,) * 3,
        scratch_shapes=[
            pltpu.VMEM((2, units, feat), BF16),
            pltpu.VMEM((2, units, feat), BF16),
            pltpu.VMEM((2, groups * slots, feat), BF16),
            pltpu.VMEM((2, groups * slots, feat), BF16),
            pltpu.VMEM((2, groups * slots, feat), BF16),
            pltpu.VMEM((groups, rows, 2 * LANES), BF16),
            pltpu.VMEM((2, groups * slots, LANES), F32),
            pltpu.VMEM((groups * slots, units), BF16),
            pltpu.VMEM((groups * slots, units), BF16),
            pltpu.SemaphoreType.DMA((2,)),
        ],
        compiler_params=pltpu.CompilerParams(vmem_limit_bytes=52 * 1024 * 1024),
        cost_estimate=pl.CostEstimate(
            flops=8 * 10**9, bytes_accessed=16 * 10**6, transcendentals=10**6
        ),
    )(where, near, over, up_t, down)


def body(sections, tokens, routes, gate_values, up_weight, down_weight, out_grad):
    tok, feat = tokens.shape[1:]
    top = routes.shape[2]
    gates = gate_values[0]
    names = routes[0].astype(BF16)
    high = lax.reduce_precision(gates, 8, 7)
    gap = jnp.zeros((tok, 16 - 2 * top), BF16)
    meta = jnp.concatenate(
        [names, names, gap, high.astype(BF16), (gates - high).astype(BF16)], axis=1
    )
    meta = jnp.pad(meta, ((0, 0), (0, LANES - meta.shape[1])))
    mine = jnp.concatenate([tokens[0], out_grad[0], meta], axis=1)

    line = gather(mine, Z_CLASSES)
    near = gather(line, Y_RINGS)
    over = send(near, flip=1)

    z_lo = lax.axis_index("dp")
    position = lax.axis_index("expert")
    where = jnp.stack([position * up_weight.shape[1], z_lo // CLASS]).astype(jnp.int32)
    keep, give, parts = run_experts(
        near, over, jnp.swapaxes(up_weight[0], 1, 2), down_weight[0], where, tok, feat
    )

    both = (keep.astype(F32) + send(give, flip=1).astype(F32)).astype(BF16)
    total = scatter_sum(both, Y_RINGS)
    lower = (position // CORES) % Z_HI == 0
    inner = jnp.where(lower, total[:tok], total[tok:])
    outer = jnp.where(lower, total[tok:], total[:tok])
    beyond = jnp.concatenate([outer[:, :feat], outer[:, 2 * feat :]], axis=1)
    beyond = send(beyond, dz=Z_LO).astype(F32)
    layer_output = (inner[:, :feat].astype(F32) + beyond[:, :feat]).astype(BF16)
    dots = inner[:, 2 * feat :].astype(F32) + beyond[:, feat:]
    gate_grad = dots[:, :top] + dots[:, top : 2 * top]
    input_grad = send_to_section_before(inner[:, feat : 2 * feat], sections).astype(
        F32
    ) + send_to_section_before(outer[:, feat : 2 * feat], sections, dz=Z_LO).astype(F32)

    shape = parts.shape
    parts = parts.reshape(-1, shape[-1])
    parts, total = lax.optimization_barrier((parts, total))
    sums = scatter_sum(parts, Z_BLOCKS).reshape(shape[1:])
    return (
        layer_output[None],
        input_grad.astype(BF16)[None],
        gate_grad[None],
        sums[0][None],
        sums[1][None],
    )


def solution(mesh):
    placed = (
        P("section", ("dp", "expert"), None),
        P("section", ("dp", "expert"), None),
        P("section", ("dp", "expert"), None),
        P("section", "expert", None, None),
        P("section", "expert", None, None),
        P("section", ("dp", "expert"), None),
    )
    return jax.shard_map(
        functools.partial(body, mesh.shape["section"]),
        mesh=mesh,
        in_specs=placed,
        out_specs=(
            P("section", ("dp", "expert"), None),
            P("section", ("dp", "expert"), None),
            P("section", ("dp", "expert"), None),
            P("section", "expert", "dp", None),
            P("section", "expert", "dp", None),
        ),
        check_vma=False,
    )
```

time: 266 us -> 280 us (1.053)
  starting transfers between devices: 132 us -> 32 us
  blocking collectives: 0 us -> 69 us
  waiting for transfers between devices: 103 us -> 137 us
  between operations: 1.03 us -> 13.9 us
    ppermute x19 -> x3, starting transfers between devices: 101 us -> 5.87 us  [send(): return lax.ppermute(block, PLANE, moved(dz, dy, flip))]
    all_gather x0 -> x1, blocking collectives: none -> 69 us  [gather(): lax.all_gather(block, PLANE, axis=0, tiled=True, axis_index_groups=rings)]
    reduce_scatter x0 -> x2, waiting for transfers between devices: none -> 56.5 us  [scatter_sum(): lax.psum_scatter(block, PLANE, scatter_dimension=0, tiled=True, axis_inde...]
    all_gather x0 -> x1, waiting for transfers between devices: none -> 46.2 us  [gather(): lax.all_gather(block, PLANE, axis=0, tiled=True, axis_index_groups=rings)]
    ppermute x19 -> x3, waiting for transfers between devices: 70.3 us -> 26.8 us  [send(): return lax.ppermute(block, PLANE, moved(dz, dy, flip))]
    ppermute x3 -> x0, waiting for transfers between devices: 31.5 us -> none  [send_in_block(): return lax.ppermute(block, PLANE, pairs)]
    ppermute x3 -> x0, starting transfers between devices: 14.8 us -> none  [send_in_block(): return lax.ppermute(block, PLANE, pairs)]
    ppermute x2, starting transfers between devices: 15.8 us -> 26.1 us  [send_to_section_before(): return lax.ppermute(block, ROUND, pairs)]
  transfers between devices with their start and end apart: 24 -> 8, of which waited for: 13 -> 7; matrix products, arithmetic and copies ran while one was open for 2% -> 1% of each run, Pallas kernels for 0% -> 0%
where the time goes in v2:
time: 280 us; the launch traced here: 277 us
  waiting for transfers between devices  137 us (49%)
  blocking collectives  69 us (25%)
  starting transfers between devices  32 us (11%)
  Pallas kernels  14.1 us (5%)
  between operations  13.9 us (5%)
  local copies, waits for them, and re-layouts  5.83 us (2%)
  other arithmetic  4.36 us (2%)
    all_gather x1, blocking collectives, gather(): lax.all_gather(block, PLANE, axis=0, tiled=True, axis_index_groups=rings)  69 us
    reduce_scatter x2, waiting for transfers between devices, scatter_sum(): lax.psum_scatter(block, PLANE, scatter_dimension=0, tiled=True, axis_inde...  56.5 us
    all_gather x1, waiting for transfers between devices, gather(): lax.all_gather(block, PLANE, axis=0, tiled=True, axis_index_groups=rings)  46.2 us
    ppermute x3, waiting for transfers between devices, send(): return lax.ppermute(block, PLANE, moved(dz, dy, flip))  26.8 us
    ppermute x2, starting transfers between devices, send_to_section_before(): return lax.ppermute(block, ROUND, pairs)  26.1 us
    pallas_call x1, Pallas kernels, run_experts(): pl.pallas_call(kernel, out_shape=(jax.ShapeDtypeStruct((rows // 2, width)...  14.1 us
    ppermute x2, waiting for transfers between devices, send_to_section_before(): return lax.ppermute(block, ROUND, pairs)  7.77 us
    ppermute x3, starting transfers between devices, send(): return lax.ppermute(block, PLANE, moved(dz, dy, flip))  5.87 us
  transfers between devices with their start and end apart: 8, of which 7 were waited for; matrix products, arithmetic and copies ran while one was open for 1% of the time, Pallas kernels for 0%

profile of v2, /device:TPU:24, one launch (start us, length us, event | category | flops | bytes accessed | tf_op | source)
XLA Modules:
  0.0 276.7 jit_solution(4540962630172340680)
XLA Ops:
  7.2 0.0 all-gather.2.cloned.1.call-start
  7.2 0.8 copy.11
  8.0 0.8 copy.12
  8.8 0.1 concatenate.9
  8.9 0.8 fusion.1
  9.7 69.0 %all_gather.6 = bf16[192,2176]{1,0:T(8,128)(2,1)} all-gather(bf16[24,2176]{1,0:T(8,128)(2,1)S(1)} %fusion.1), channel_id=1, replica_groups={{0,64,128,192,2,66,130,194},{1,65,129,193,3,67,131,195},{4,68,132,196,6..., dimensions={0}, use_global_device_ids=true | all-gather | bytes 940032 | tf_op jit(solution)/shard_map/all_gather | solution.py:50
  78.7 0.0 all-gather.2.cloned.1.call-update
  78.8 0.0 reduce-scatter.3.cloned.1.call-start
  78.8 46.2 %all-gather.2.cloned.1.call-done.near_ref = bf16[768,2176]{1,0:T(8,128)(2,1)} async-done(((bf16[192,2176]{1,0:T(8,128)(2,1)}), bf16[768,2176]{1,0:T(8,128)(2,1)}) %all-gather.2.cloned.1.call-update) | async-done | bytes 3342352 | tf_op jit(solution)/shard_map/all_gather | solution.py:50
  125.0 1.9 collective-permute-start
  127.0 0.1 pad_add_fusion.place_ref
  127.1 6.0 %collective-permute-done.over_ref = bf16[768,2176]{1,0:T(8,128)(2,1)S(1)} collective-permute-done((bf16[768,2176]{1,0:T(8,128)(2,1)}, bf16[768,2176]{1,0:T(8,128)(2,1)S(1)}, u32[]{:S(2)}, u32[]{:S(2)}) %collective-permute-start) | collective-permute-done | bytes 3342368 | tf_op jit(solution)/shard_map/ppermute | solution.py:36
  133.1 1.7 copy-done
  134.8 14.1 %shard_map.101 = (bf16[192,2176]{1,0:T(8,128)(2,1)S(1)}, bf16[192,2176]{1,0:T(8,128)(2,1)S(1)}, bf16[4,2,2,64,704]{4,3,2,1,0:T(8,128)(2,1)}) custom-call(s32[2]{0:T(128)S(1)} %pad_add_fusion.place_ref, bf16[768,2176]{1,0:T(8,128)(2,1)} %all-gather.2.cloned.1.call-done.near_ref, bf16[768,2176]{1,0:T(8,128)(2,1)} %copy-done, bf16[2,704,1024]{2,1,0:T(8,128)(2,1)} %bitcast.27, ...), custom_call_target="tpu_custom_call" | custom-call | flops 8000000000 | bytes 16000000 | tf_op jit(solution)/shard_map/pallas_call | solution.py:182
  148.9 2.0 collective-permute-start.1
  151.0 2.2 collective-permute-done.1
  153.2 1.1 add_convert_fusion
  154.3 0.0 reduce-scatter.3.cloned.1.call-update
  154.3 0.0 reduce-scatter.5.cloned.1.call-start
  154.4 42.6 %reduce-scatter.3.cloned.1.call-done = bf16[48,2176]{1,0:T(8,128)(2,1)} async-done(((bf16[192,2176]{1,0:T(8,128)(2,1)}), bf16[48,2176]{1,0:T(8,128)(2,1)}) %reduce-scatter.3.cloned.1.call-update) | async-done | bytes 208912 | tf_op jit(solution)/shard_map/reduce_scatter | solution.py:54
  197.0 1.0 broadcast_select_fusion.1
  198.0 2.6 collective-permute-start.3
  200.7 23.4 %collective-permute-start.4 = (bf16[24,1024]{1,0:T(8,128)(2,1)S(1)}, bf16[24,1024]{1,0:T(8,128)(2,1)S(1)}, u32[]{:S(2)}, u32[]{:S(2)}) collective-permute-start(bf16[24,1024]{1,0:T(8,128)(2,1)S(1)} %get-tuple-element.22), channel_id=1, source_target_pairs={{0,770},{1,771},{4,774},{5,775},{8,778},{9,779},{12,782},{13,783},... | collective-permute-start | bytes 147464 | tf_op jit(solution)/shard_map/ppermute | solution.py:66
  224.1 1.9 collective-permute-start.2
  226.1 7.8 %collective-permute-done.4 = bf16[24,1024]{1,0:T(8,128)(2,1)S(1)} collective-permute-done((bf16[24,1024]{1,0:T(8,128)(2,1)S(1)}, bf16[24,1024]{1,0:T(8,128)(2,1)S(1)}, u32[]{:S(2)}, u32[]{:S(2)}) %collective-permute-start.4) | collective-permute-done | bytes 49184 | tf_op jit(solution)/shard_map/ppermute | solution.py:66
  233.8 0.6 fusion.3
  234.5 18.6 %collective-permute-done.2 = bf16[24,1152]{1,0:T(8,128)(2,1)S(1)} collective-permute-done((bf16[24,1152]{1,0:T(8,128)(2,1)S(1)}, bf16[24,1152]{1,0:T(8,128)(2,1)S(1)}, u32[]{:S(2)}, u32[]{:S(2)}) %collective-permute-start.2) | collective-permute-done | bytes 55328 | tf_op jit(solution)/shard_map/ppermute | solution.py:36
  253.1 0.1 fusion.6
  253.2 0.7 copy.13
  253.8 0.6 fusion.4
  254.5 13.9 %reduce-scatter.5.cloned.1.call-done = bf16[256,704]{1,0:T(8,128)(2,1)} async-done(((bf16[1024,704]{1,0:T(8,128)(2,1)}), bf16[256,704]{1,0:T(8,128)(2,1)}) %reduce-scatter.5.cloned.1.call-update) | async-done | bytes 360464 | tf_op jit(solution)/shard_map/reduce_scatter | solution.py:54
  268.4 1.8 fusion.7
  (12 shorter events, 0.1 us)
Async XLA Ops:
  7.2 117.9 %all-gather.2.cloned.1.call-start = ((), (), s32[]{:S(2)}) async-start(), calls=%async_computation.2 | async-start | bytes 4177920 | tf_op jit(solution)/shard_map/all_gather | solution.py:50
  78.8 118.2 %reduce-scatter.3.cloned.1.call-start = ((), (), s32[]{:S(2)}) async-start(), calls=%async_computation.3 | async-start | bytes 1044480 | tf_op jit(solution)/shard_map/reduce_scatter | solution.py:54
  125.0 8.0 %collective-permute-start = (bf16[768,2176]{1,0:T(8,128)(2,1)}, bf16[768,2176]{1,0:T(8,128)(2,1)S(1)}, u32[]{:S(2)}, u32[]{:S(2)}) collective-permute-start(bf16[768,2176]{1,0:T(8,128)(2,1)} %all-gather.2.cloned.1.call-done.near_ref), channel_id=1, source_target_pairs={{0,1},{1,0},{4,5},{5,4},{8,9},{9,8},{12,13},{13,12},{16,17},{17,16... | collective-permute-start | bytes 10027016 | tf_op jit(solution)/shard_map/ppermute | solution.py:36
  133.1 1.7 copy-start
  148.9 4.2 %collective-permute-start.1 = (bf16[192,2176]{1,0:T(8,128)(2,1)S(1)}, bf16[192,2176]{1,0:T(8,128)(2,1)S(1)}, u32[]{:S(2)}, u32[]{:S(2)}) collective-permute-start(bf16[192,2176]{1,0:T(8,128)(2,1)S(1)} %get-tuple-element.10), channel_id=1, source_target_pairs={{0,1},{1,0},{4,5},{5,4},{8,9},{9,8},{12,13},{13,12},{16,17},{17,16... | collective-permute-start | bytes 2506760 | tf_op jit(solution)/shard_map/ppermute | solution.py:36
  154.3 114.1 %reduce-scatter.5.cloned.1.call-start = ((), (), s32[]{:S(2)}) async-start(), calls=%async_computation.4 | async-start | bytes 1966080 | tf_op jit(solution)/shard_map/reduce_scatter | solution.py:54
  198.0 28.0 %collective-permute-start.3 = (bf16[24,1024]{1,0:T(8,128)(2,1)S(1)}, bf16[24,1024]{1,0:T(8,128)(2,1)S(1)}, u32[]{:S(2)}, u32[]{:S(2)}) collective-permute-start(bf16[24,1024]{1,0:T(8,128)(2,1)S(1)} %slice.72), channel_id=1, source_target_pairs={{0,768},{1,769},{4,772},{5,773},{8,776},{9,777},{12,780},{13,781},... | collective-permute-start | bytes 147464 | tf_op jit(solution)/shard_map/ppermute | solution.py:66
  200.7 33.2 %collective-permute-start.4 = (bf16[24,1024]{1,0:T(8,128)(2,1)S(1)}, bf16[24,1024]{1,0:T(8,128)(2,1)S(1)}, u32[]{:S(2)}, u32[]{:S(2)}) collective-permute-start(bf16[24,1024]{1,0:T(8,128)(2,1)S(1)} %get-tuple-element.22), channel_id=1, source_target_pairs={{0,770},{1,771},{4,774},{5,775},{8,778},{9,779},{12,782},{13,783},... | collective-permute-start | bytes 147464 | tf_op jit(solution)/shard_map/ppermute | solution.py:66
  224.1 28.9 %collective-permute-start.2 = (bf16[24,1152]{1,0:T(8,128)(2,1)S(1)}, bf16[24,1152]{1,0:T(8,128)(2,1)S(1)}, u32[]{:S(2)}, u32[]{:S(2)}) collective-permute-start(bf16[24,1152]{1,0:T(8,128)(2,1)S(1)} %pad_maximum_fusion), channel_id=1, source_target_pairs={{0,2},{1,3},{4,6},{5,7},{8,10},{9,11},{12,14},{13,15},{16,18},{17,... | collective-permute-start | bytes 165896 | tf_op jit(solution)/shard_map/ppermute | solution.py:36
Sparse Core Ops, SparseCore 0:
  78.9 46.1 all-gather.1
  154.4 42.4 reduce-scatter.2
  200.8 67.5 reduce-scatter.4

commit v3 on v2

v3 whole, which is shorter than its diff:
```python
import functools

import jax
import jax.numpy as jnp
from jax import lax
from jax.experimental import pallas as pl
from jax.experimental.pallas import tpu as pltpu
from jax.sharding import PartitionSpec as P

PLANE = ("dp", "expert")
ROUND = ("section", "dp", "expert")
LANES = 128
GATES_AT = 32
CAPACITY = 6
F32 = jnp.float32
BF16 = jnp.bfloat16

Z_LO, Y, Z_HI, CORES = 16, 4, 2, 2
Z = Z_LO * Z_HI
CLASS = 4
GROUPS = Z_LO // CLASS


def place(z, y, core):
    return (z % Z_LO) * (Y * Z_HI * CORES) + y * (Z_HI * CORES) + (z // Z_LO) * CORES + core


def moved(dz=0, dy=0, flip=0, block_flip=0):
    return [
        (place(z, y, c), place(((z ^ block_flip) + dz) % Z, (y + dy) % Y, c ^ flip))
        for z in range(Z)
        for y in range(Y)
        for c in range(CORES)
    ]


def send(block, **route):
    return lax.ppermute(block, PLANE, moved(**route))


LINES = [(y, c) for y in range(Y) for c in range(CORES)]
Z_CLASSES = [
    [place(z, y, c) for z in range(r, Z, CLASS)] for r in range(CLASS) for y, c in LINES
]
Y_RINGS = [[place(z, y, c) for y in range(Y)] for z in range(Z) for c in range(CORES)]


def gather(block, rings):
    return lax.all_gather(block, PLANE, axis=0, tiled=True, axis_index_groups=rings)


def send_to_section_before(block, sections, **route):
    plane = Z * Y * CORES
    pairs = [
        (s * plane + a, ((s - 1) % sections) * plane + b)
        for s in range(sections)
        for a, b in moved(**route)
    ]
    return lax.ppermute(block, ROUND, pairs)


def dot(a, b, over):
    return lax.dot_general(a, b, (over, ((), ())), preferred_element_type=F32)


NN = ((1,), (0,))
NT = ((1,), (1,))
TN = ((0,), (0,))


def constants(rows, tok, slots, experts, top):
    lanes = experts * slots
    r_row = lax.broadcasted_iota(jnp.int32, (rows, rows), 0)
    r_col = lax.broadcasted_iota(jnp.int32, (rows, rows), 1)
    before = (r_col <= r_row) & (r_col // tok == r_row // tok)
    m_row = lax.broadcasted_iota(jnp.int32, (LANES, lanes), 0)
    m_col = lax.broadcasted_iota(jnp.int32, (LANES, lanes), 1)
    row = lax.broadcasted_iota(jnp.int32, (rows, lanes), 0)
    lane = lax.broadcasted_iota(jnp.int32, (rows, lanes), 1)
    return (
        jnp.where(before, 1.0, 0.0).astype(BF16),
        jnp.where(m_row // top == m_col // slots, 1.0, 0.0).astype(BF16),
        (lane % slots - row // tok * CAPACITY + 1).astype(F32),
    )


def slot_picks(meta, names, top, consts):
    before, spread, wanted = consts
    lane = lax.broadcasted_iota(jnp.int32, meta.shape, 1)
    name = jnp.full(meta.shape, -1.0, F32)
    for e, value in enumerate(names):
        name = jnp.where((lane >= e * top) & (lane < (e + 1) * top), value, name)
    hit = jnp.where(meta.astype(F32) == name, 1.0, 0.0).astype(BF16)
    named = dot(hit, spread, NN)
    rank = dot(before, named.astype(BF16), NN)
    return jnp.where((named > 0.5) & (rank == wanted), 1.0, 0.0).astype(BF16)


def slot_gate(m, name, top):
    lane = lax.broadcasted_iota(jnp.int32, m.shape, 1)
    gates = pltpu.roll(m, LANES - GATES_AT, 1)
    match = (m == name) & (lane < 2 * top)
    return match, jnp.sum(jnp.where(match, gates, 0.0), axis=1, keepdims=True)


def through_expert(x, grad, up, down):
    hidden = dot(x, up, NT)
    logistic = 1.0 / (1.0 + jnp.exp(-hidden))
    slope = logistic * (1.0 + hidden * (1.0 - logistic))
    act = (hidden * logistic).astype(BF16)
    return act, (dot(grad, down, NT) * slope).astype(BF16)


def experts_kernel(
    place_ref, line, left, right, far_left, far_right,
    up_own, down_own, up_other, down_other, back_out, keep_out, give_out,
    rows_ref, up_ref, down_ref, xs, gs, us, picked, metas, acts, hgs, result_ref, sums,
    landed, arrived, *, tok, feat, local, top,
):
    experts = CORES * local
    names = [place_ref[e].astype(F32) for e in range(experts)]
    block_at, y_at, spot = place_ref[experts], place_ref[experts + 1], place_ref[experts + 2]
    span = GROUPS * tok
    landings = [
        pltpu.make_async_copy(line, rows_ref.at[0], landed.at[0]),
        pltpu.make_async_copy(left, rows_ref.at[1], landed.at[1]),
        pltpu.make_async_copy(far_left, rows_ref.at[2, pl.ds(0, span)], landed.at[2]),
        pltpu.make_async_copy(far_right, rows_ref.at[2, pl.ds(span, span)], landed.at[3]),
        pltpu.make_async_copy(right, rows_ref.at[3], landed.at[4]),
    ]
    copies = []
    for a, (up, down) in enumerate(((up_own, down_own), (up_other, down_other))):
        here = pl.ds(a * local, local)
        copies.append(pltpu.make_async_copy(up, up_ref.at[here], arrived.at[0, a]))
        copies.append(pltpu.make_async_copy(down, down_ref.at[here], arrived.at[1, a]))
    for copy in landings + copies:
        copy.start()
    sources = [(d, h * span) for d in range(Y) for h in range(Z_HI)]
    rows = len(sources) * tok
    slots = len(sources) * CAPACITY
    consts = constants(rows, tok, slots, experts, top)
    for copy in landings:
        copy.wait()
    for g in range(GROUPS):
        block = jnp.concatenate(
            [rows_ref[d, start + g * tok : start + (g + 1) * tok, :] for d, start in sources],
            axis=0,
        )
        picks = slot_picks(block[:, 2 * feat :], names, top, consts)
        picked[g] = picks
        gathered = dot(picks, block, TN)
        for e in range(experts):
            here = slice(g * slots, (g + 1) * slots)
            part = gathered[e * slots : (e + 1) * slots]
            match, gate = slot_gate(part[:, 2 * feat :], names[e], top)
            grad = part[:, feat : 2 * feat]
            xs[e, here, :] = part[:, :feat].astype(BF16)
            us[e, here, :] = grad.astype(BF16)
            gs[e, here, :] = (gate * grad).astype(BF16)
            metas[e, here, :] = jnp.where(match, gate, 0.0)
    s_lane = lax.broadcasted_iota(jnp.int32, (slots, LANES), 1)
    own = pl.ds(pl.multiple_of(block_at * slots, slots), slots)
    columns = feat // GROUPS
    cols = pl.ds(pl.multiple_of(block_at * columns, columns), columns)
    each = columns // CLASS
    back = []
    for a in range(CORES):
        copies[2 * a].wait()
        copies[2 * a + 1].wait()
        for j in range(local):
            e = a * local + j
            act, hg = through_expert(xs[e], gs[e], up_ref[e], down_ref[e])
            acts[...] = act
            hgs[...] = hg
            kept = metas[e, own, :]
            gate = jnp.max(kept, axis=1, keepdims=True)
            out = dot(acts[own, :], down_ref[e], NN).astype(BF16).astype(F32)
            dots = jnp.sum(us[e, own, :].astype(F32) * out, axis=1, keepdims=True)
            high = dots.astype(BF16).astype(F32)
            d = jnp.where(kept > 0.0, jnp.where(s_lane < top, high, dots - high), 0.0)
            rg = dot(hgs[own, :], up_ref[e], NN).astype(BF16)
            back.append(jnp.concatenate([(gate * out).astype(BF16), d.astype(BF16), rg], axis=1))
            for m, (side, value) in enumerate(((xs, hgs), (gs, acts))):
                sums[...] = dot(side[e, :, cols], value[...], TN).astype(BF16)
                for q in range(CLASS):
                    take = pl.ds(pl.multiple_of((spot ^ q) * each, each), each)
                    (keep_out, give_out)[a][q % 2, q // 2, m, j] = sums[take, :]
    stacked = jnp.concatenate(back, axis=0)
    result_ref[...] = dot(picked[block_at], stacked, NN).astype(BF16)
    share = rows // Y
    for y in range(Y):
        start = pl.multiple_of(((y_at + Y - y) % Y) * share, share)
        back_out[y * share : (y + 1) * share, :] = result_ref[pl.ds(start, share), :]


VMEM = pl.BlockSpec(memory_space=pltpu.VMEM)
HBM = pl.BlockSpec(memory_space=pltpu.HBM)
SCALARS = pl.BlockSpec(memory_space=pltpu.SMEM)


def run_experts(pieces, weights, where, tok, feat, top):
    local, units, _ = weights[0].shape
    width = pieces[0].shape[1]
    experts = CORES * local
    rows = pieces[0].shape[0] // GROUPS * Y
    slots = rows // tok * CAPACITY
    parts = jax.ShapeDtypeStruct((2, 2, 2, local, feat // Z_LO, units), BF16)
    return pl.pallas_call(
        functools.partial(experts_kernel, tok=tok, feat=feat, local=local, top=top),
        out_shape=(
            jax.ShapeDtypeStruct((rows, width), BF16),
            parts,
            parts,
        ),
        in_specs=[SCALARS] + [HBM] * (len(pieces) + len(weights)),
        out_specs=(VMEM,) * 3,
        scratch_shapes=[
            pltpu.VMEM((Y, pieces[0].shape[0], width), BF16),
            pltpu.VMEM((experts, units, feat), BF16),
            pltpu.VMEM((experts, units, feat), BF16),
            pltpu.VMEM((experts, GROUPS * slots, feat), BF16),
            pltpu.VMEM((experts, GROUPS * slots, feat), BF16),
            pltpu.VMEM((experts, GROUPS * slots, feat), BF16),
            pltpu.VMEM((GROUPS, rows, experts * slots), BF16),
            pltpu.VMEM((experts, GROUPS * slots, LANES), F32),
            pltpu.VMEM((GROUPS * slots, units), BF16),
            pltpu.VMEM((GROUPS * slots, units), BF16),
            pltpu.VMEM((rows, width), BF16),
            pltpu.VMEM((feat // GROUPS, units), BF16),
            pltpu.SemaphoreType.DMA((len(pieces),)),
            pltpu.SemaphoreType.DMA((2, CORES)),
        ],
        compiler_params=pltpu.CompilerParams(vmem_limit_bytes=44 * 1024 * 1024),
        cost_estimate=pl.CostEstimate(
            flops=12 * 10**9, bytes_accessed=20 * 10**6, transcendentals=10**6
        ),
    )(where, *pieces, *weights)


def both_halves(kept, got):
    return (kept.astype(F32) + got.astype(F32)).astype(BF16)


def body(sections, tokens, routes, gate_values, up_weight, down_weight, out_grad):
    tok, feat = tokens.shape[1:]
    top = routes.shape[2]
    gates = gate_values[0]
    names = routes[0].astype(BF16)
    high = lax.reduce_precision(gates, 8, 7)
    copies = CORES * up_weight.shape[1]
    gap = jnp.zeros((tok, GATES_AT - copies * top), BF16)
    meta = jnp.concatenate(
        [names] * copies + [gap, high.astype(BF16), (gates - high).astype(BF16)], axis=1
    )
    meta = jnp.pad(meta, ((0, 0), (0, LANES - meta.shape[1])))
    mine = jnp.concatenate([tokens[0], out_grad[0], meta], axis=1)

    z_lo = lax.axis_index("dp")
    position = lax.axis_index("expert")
    local = up_weight.shape[1]
    other = position + 1 - 2 * (position % CORES)
    first = [p * local + j for p in (position, other) for j in range(local)]
    y_at = position // (CORES * Z_HI)
    where = jnp.stack(first + [z_lo // CLASS, y_at, z_lo % CLASS]).astype(jnp.int32)
    up_t, down = jnp.swapaxes(up_weight[0], 1, 2), down_weight[0]

    line = gather(mine, Z_CLASSES)
    middle = line.shape[0] // 2
    left, right = send(line, dy=1), send(line, dy=-1)
    far_left, far_right = send(left[:middle], dy=1), send(right[middle:], dy=-1)
    weights = [up_t, down]
    up_t, down, _ = lax.optimization_barrier((up_t, down, line))
    weights = weights + [send(up_t, flip=1), send(down, flip=1)]
    back, keep, give = run_experts(
        [line, left, right, far_left, far_right], weights, where, tok, feat, top
    )

    share = back.shape[0] // Y
    spread = lax.all_to_all(back, PLANE, 0, 0, tiled=True, axis_index_groups=Y_RINGS)
    total = jnp.sum(spread.reshape(Y, share, -1).astype(F32), axis=0).astype(BF16)
    below = (position // CORES) % Z_HI == 0
    inner = jnp.where(below, total[:tok], total[tok:])
    outer = jnp.where(below, total[tok:], total[:tok])

    got = send(give, flip=1)
    give = both_halves(keep[1], got[1])
    keep = both_halves(keep[0], got[0])
    got = send(give, block_flip=1)
    give = both_halves(keep[1], got[1])
    keep = both_halves(keep[0], got[0])
    last = send(give, block_flip=2)
    beyond = send(outer, dz=Z_LO)
    beyond, last = lax.optimization_barrier((beyond, last))
    added = inner.astype(F32) + beyond.astype(F32)
    dots = added[:, feat : feat + LANES]
    gate_grad = dots[:, :top] + dots[:, top : 2 * top]
    input_grad = send_to_section_before(added[:, feat + LANES :].astype(BF16), sections)
    sums = both_halves(keep, last)
    return (
        added[:, :feat].astype(BF16)[None],
        input_grad[None],
        gate_grad[None],
        sums[0][None],
        sums[1][None],
    )


def solution(mesh):
    placed = (
        P("section", ("dp", "expert"), None),
        P("section", ("dp", "expert"), None),
        P("section", ("dp", "expert"), None),
        P("section", "expert", None, None),
        P("section", "expert", None, None),
        P("section", ("dp", "expert"), None),
    )
    return jax.shard_map(
        functools.partial(body, mesh.shape["section"]),
        mesh=mesh,
        in_specs=placed,
        out_specs=(
            P("section", ("dp", "expert"), None),
            P("section", ("dp", "expert"), None),
            P("section", ("dp", "expert"), None),
            P("section", "expert", "dp", None),
            P("section", "expert", "dp", None),
        ),
        check_vma=False,
    )
```

time: 280 us -> 214 us (0.76)
  the two profiles are of different devices: /device:TPU:24 before, /device:TPU:38 now
where the time goes in v3:
time: 214 us; the launch traced here: 213 us
  waiting for transfers between devices  78.9 us (37%)
  blocking collectives  62 us (29%)
  starting transfers between devices  49.1 us (23%)
  Pallas kernels  12.8 us (6%)
  local copies, waits for them, and re-layouts  7.79 us (4%)
    ppermute x10, waiting for transfers between devices, send(): return lax.ppermute(block, PLANE, moved(**route))  62.1 us
    all_gather x1, blocking collectives, gather(): lax.all_gather(block, PLANE, axis=0, tiled=True, axis_index_groups=rings)  62 us
    ppermute x10, starting transfers between devices, send(): return lax.ppermute(block, PLANE, moved(**route))  42.9 us
    all_to_all x1, waiting for transfers between devices, body(): lax.all_to_all(back, PLANE, 0, 0, tiled=True, axis_index_groups=Y_RINGS)  13.1 us
    pallas_call x1, Pallas kernels, run_experts(): pl.pallas_call(functools.partial(experts_kernel, tok=tok, feat=feat, loca...  12.8 us
    unnamed x6, local copies, waits for them, and re-layouts  4.61 us
  transfers between devices with their start and end apart: 12, of which 8 were waited for; matrix products, arithmetic and copies ran while one was open for 1% of the time, Pallas kernels for 0%

profile of v3, /device:TPU:38, one launch (start us, length us, event | category | flops | bytes accessed | tf_op | source)
XLA Modules:
  0.0 213.4 jit_solution(16259943243586014106)
XLA Ops:
  0.6 0.8 copy.13
  1.4 0.8 copy.14
  2.3 0.8 fusion.7
  3.1 62.0 %all_gather.3.line = bf16[192,2176]{1,0:T(8,128)(2,1)S(1)} all-gather(bf16[24,2176]{1,0:T(8,128)(2,1)S(1)} %fusion.7), channel_id=1, replica_groups={{0,64,128,192,2,66,130,194},{1,65,129,193,3,67,131,195},{4,68,132,196,6..., dimensions={0}, use_global_device_ids=true | all-gather | bytes 940032 | tf_op jit(solution)/shard_map/all_gather | solution.py:49
  65.1 1.9 collective-permute-start.4
  67.1 2.4 %collective-permute-start.5 = (bf16[2,704,1024]{2,1,0:T(8,128)(2,1)}, bf16[2,704,1024]{2,1,0:T(8,128)(2,1)}, u32[]{:S(2)}, u32[]{:S(2)}) collective-permute-start(bf16[2,704,1024]{2,1,0:T(8,128)(2,1)} %bitcast.48), channel_id=1, source_target_pairs={{0,1},{1,0},{4,5},{5,4},{8,9},{9,8},{12,13},{13,12},{16,17},{17,16... | collective-permute-start | bytes 8650760 | tf_op jit(solution)/shard_map/ppermute | solution.py:38
  69.5 4.9 %collective-permute-start.1 = (bf16[192,2176]{1,0:T(8,128)(2,1)S(1)}, bf16[192,2176]{1,0:T(8,128)(2,1)S(1)}, u32[]{:S(2)}, u32[]{:S(2)}) collective-permute-start(bf16[192,2176]{1,0:T(8,128)(2,1)S(1)} %all_gather.3.line), channel_id=1, source_target_pairs={{0,12},{1,13},{4,0},{5,1},{8,4},{9,5},{12,8},{13,9},{16,28},{17,29... | collective-permute-start | bytes 2506760 | tf_op jit(solution)/shard_map/ppermute | solution.py:38
  74.4 1.9 collective-permute-start
  76.3 16.1 %collective-permute-done.1.right = bf16[192,2176]{1,0:T(8,128)(2,1)S(1)} collective-permute-done((bf16[192,2176]{1,0:T(8,128)(2,1)S(1)}, bf16[192,2176]{1,0:T(8,128)(2,1)S(1)}, u32[]{:S(2)}, u32[]{:S(2)}) %collective-permute-start.1) | collective-permute-done | bytes 835616 | tf_op jit(solution)/shard_map/ppermute | solution.py:38
  92.4 0.8 slice.82
  93.2 5.6 %collective-permute-start.3 = (bf16[96,2176]{1,0:T(8,128)(2,1)}, bf16[96,2176]{1,0:T(8,128)(2,1)S(1)}, u32[]{:S(2)}, u32[]{:S(2)}) collective-permute-start(bf16[96,2176]{1,0:T(8,128)(2,1)} %slice.82), channel_id=1, source_target_pairs={{0,12},{1,13},{4,0},{5,1},{8,4},{9,5},{12,8},{13,9},{16,28},{17,29... | collective-permute-start | bytes 1253384 | tf_op jit(solution)/shard_map/ppermute | solution.py:38
  98.8 0.8 slice.81
  99.6 1.9 collective-permute-start.2
  101.7 5.7 %collective-permute-done.3.far_right = bf16[96,2176]{1,0:T(8,128)(2,1)S(1)} collective-permute-done((bf16[96,2176]{1,0:T(8,128)(2,1)}, bf16[96,2176]{1,0:T(8,128)(2,1)S(1)}, u32[]{:S(2)}, u32[]{:S(2)}) %collective-permute-start.3) | collective-permute-done | bytes 417824 | tf_op jit(solution)/shard_map/ppermute | solution.py:38
  107.3 6.0 %collective-permute-done.2.far_left = bf16[96,2176]{1,0:T(8,128)(2,1)S(1)} collective-permute-done((bf16[96,2176]{1,0:T(8,128)(2,1)}, bf16[96,2176]{1,0:T(8,128)(2,1)S(1)}, u32[]{:S(2)}, u32[]{:S(2)}) %collective-permute-start.2) | collective-permute-done | bytes 417824 | tf_op jit(solution)/shard_map/ppermute | solution.py:38
  113.4 1.8 copy-done
  115.2 12.8 %shard_map.101 = (bf16[192,2176]{1,0:T(8,128)(2,1)}, bf16[2,2,2,2,64,704]{5,4,3,2,1,0:T(8,128)(2,1)S(1)}, bf16[2,2,2,2,64,704]{5,4,3,2,1,0:T(8,128)(2,1)S(1)}) custom-call(s32[7]{0:T(128)S(1)} %stack.31.place_ref, bf16[192,2176]{1,0:T(8,128)(2,1)S(1)} %all_gather.3.line, bf16[192,2176]{1,0:T(8,128)(2,1)S(1)} %collective-permute-done.left, ...), custom_call_target="tpu_custom_call" | custom-call | flops 12000000000 | bytes 20000000 | tf_op jit(solution)/shard_map/pallas_call | solution.py:208
  128.0 1.9 collective-permute-start.7
  130.0 3.4 %collective-permute-done.7 = bf16[2,2,2,2,64,704]{5,4,3,2,1,0:T(8,128)(2,1)S(1)} collective-permute-done((bf16[2,2,2,2,64,704]{5,4,3,2,1,0:T(8,128)(2,1)S(1)}, bf16[2,2,2,2,64,704]{5,4,3,2,1,0:T(8,128)(2,1)S(1)}, u32[]{:S(2)}, u32[]{:S(2)}) %collective-permute-start.7) | collective-permute-done | bytes 1441824 | tf_op jit(solution)/shard_map/ppermute | solution.py:38
  133.8 7.5 %collective-permute-start.8 = (bf16[2,2,2,64,704]{4,3,2,1,0:T(8,128)(2,1)S(1)}, bf16[2,2,2,64,704]{4,3,2,1,0:T(8,128)(2,1)S(1)}, u32[]{:S(2)}, u32[]{:S(2)}) collective-permute-start(bf16[2,2,2,64,704]{4,3,2,1,0:T(8,128)(2,1)S(1)} %get-tuple-element.27), channel_id=1, source_target_pairs={{0,16},{1,17},{4,20},{5,21},{8,24},{9,25},{12,28},{13,29},{16,0},{... | collective-permute-start | bytes 2162696 | tf_op jit(solution)/shard_map/ppermute | solution.py:38
  141.3 3.5 %all-to-all-start = ((bf16[4,48,2176]{2,1,0:T(8,128)(2,1)}), bf16[4,48,2176]{2,1,0:T(8,128)(2,1)S(1)}, u32[]{:S(2)}, u32[]{:S(2)}) async-start(bf16[4,48,2176]{2,1,0:T(8,128)(2,1)} %bitcast.15), calls=%async_computation | async-start | bytes 1671168 | tf_op jit(solution)/shard_map/all_to_all | solution.py:279
  144.9 13.1 %all-to-all-done = bf16[4,48,2176]{2,1,0:T(8,128)(2,1)S(1)} async-done(((bf16[4,48,2176]{2,1,0:T(8,128)(2,1)}), bf16[4,48,2176]{2,1,0:T(8,128)(2,1)S(1)}, u32[]{:S(2)}, u32[]{:S(2)}) %all-to-all-start) | async-done | bytes 835616 | tf_op jit(solution)/shard_map/all_to_all | solution.py:279
  158.1 1.1 collective-permute-done.8
  159.2 1.9 collective-permute-start.9
  161.2 12.8 %collective-permute-start.6 = (bf16[24,2176]{1,0:T(8,128)(2,1)S(1)}, bf16[24,2176]{1,0:T(8,128)(2,1)S(1)}, u32[]{:S(2)}, u32[]{:S(2)}) collective-permute-start(bf16[24,2176]{1,0:T(8,128)(2,1)S(1)} %broadcast_select_fusion), channel_id=1, source_target_pairs={{0,2},{1,3},{4,6},{5,7},{8,10},{9,11},{12,14},{13,15},{16,18},{17,... | collective-permute-start | bytes 313352 | tf_op jit(solution)/shard_map/ppermute | solution.py:38
  174.1 29.9 %collective-permute-done.6 = bf16[24,2176]{1,0:T(8,128)(2,1)S(1)} collective-permute-done((bf16[24,2176]{1,0:T(8,128)(2,1)S(1)}, bf16[24,2176]{1,0:T(8,128)(2,1)S(1)}, u32[]{:S(2)}, u32[]{:S(2)}) %collective-permute-start.6) | collective-permute-done | bytes 104480 | tf_op jit(solution)/shard_map/ppermute | solution.py:38
  204.0 0.6 fusion.12
  204.8 0.8 fusion.11
  205.6 2.7 %collective-permute-start.10 = (bf16[24,1024]{1,0:T(8,128)(2,1)S(1)}, bf16[24,1024]{1,0:T(8,128)(2,1)S(1)}, u32[]{:S(2)}, u32[]{:S(2)}) collective-permute-start(bf16[24,1024]{1,0:T(8,128)(2,1)S(1)} %get-tuple-element.30), channel_id=1, source_target_pairs={{0,768},{1,769},{4,772},{5,773},{8,776},{9,777},{12,780},{13,781},... | collective-permute-start | bytes 147464 | tf_op jit(solution)/shard_map/ppermute | solution.py:59
  208.4 0.7 copy.15
  209.0 3.7 %collective-permute-done.10 = bf16[24,1024]{1,0:T(8,128)(2,1)S(1)} collective-permute-done((bf16[24,1024]{1,0:T(8,128)(2,1)S(1)}, bf16[24,1024]{1,0:T(8,128)(2,1)S(1)}, u32[]{:S(2)}, u32[]{:S(2)}) %collective-permute-start.10) | collective-permute-done | bytes 49184 | tf_op jit(solution)/shard_map/ppermute | solution.py:59
  212.7 0.6 copy.17
  (17 shorter events, 1.2 us)
Async XLA Ops:
  65.1 48.2 %collective-permute-start.4 = (bf16[2,704,1024]{2,1,0:T(8,128)(2,1)}, bf16[2,704,1024]{2,1,0:T(8,128)(2,1)}, u32[]{:S(2)}, u32[]{:S(2)}) collective-permute-start(bf16[2,704,1024]{2,1,0:T(8,128)(2,1)} %bitcast.43), channel_id=1, source_target_pairs={{0,1},{1,0},{4,5},{5,4},{8,9},{9,8},{12,13},{13,12},{16,17},{17,16... | collective-permute-start | bytes 8650760 | tf_op jit(solution)/shard_map/ppermute | solution.py:38
  67.1 46.3 %collective-permute-start.5 = (bf16[2,704,1024]{2,1,0:T(8,128)(2,1)}, bf16[2,704,1024]{2,1,0:T(8,128)(2,1)}, u32[]{:S(2)}, u32[]{:S(2)}) collective-permute-start(bf16[2,704,1024]{2,1,0:T(8,128)(2,1)} %bitcast.48), channel_id=1, source_target_pairs={{0,1},{1,0},{4,5},{5,4},{8,9},{9,8},{12,13},{13,12},{16,17},{17,16... | collective-permute-start | bytes 8650760 | tf_op jit(solution)/shard_map/ppermute | solution.py:38
  69.5 22.9 %collective-permute-start.1 = (bf16[192,2176]{1,0:T(8,128)(2,1)S(1)}, bf16[192,2176]{1,0:T(8,128)(2,1)S(1)}, u32[]{:S(2)}, u32[]{:S(2)}) collective-permute-start(bf16[192,2176]{1,0:T(8,128)(2,1)S(1)} %all_gather.3.line), channel_id=1, source_target_pairs={{0,12},{1,13},{4,0},{5,1},{8,4},{9,5},{12,8},{13,9},{16,28},{17,29... | collective-permute-start | bytes 2506760 | tf_op jit(solution)/shard_map/ppermute | solution.py:38
  74.4 24.4 %collective-permute-start = (bf16[192,2176]{1,0:T(8,128)(2,1)S(1)}, bf16[192,2176]{1,0:T(8,128)(2,1)S(1)}, u32[]{:S(2)}, u32[]{:S(2)}) collective-permute-start(bf16[192,2176]{1,0:T(8,128)(2,1)S(1)} %all_gather.3.line), channel_id=1, source_target_pairs={{0,4},{1,5},{4,8},{5,9},{8,12},{9,13},{12,0},{13,1},{16,20},{17,21... | collective-permute-start | bytes 2506760 | tf_op jit(solution)/shard_map/ppermute | solution.py:38
  93.2 14.1 %collective-permute-start.3 = (bf16[96,2176]{1,0:T(8,128)(2,1)}, bf16[96,2176]{1,0:T(8,128)(2,1)S(1)}, u32[]{:S(2)}, u32[]{:S(2)}) collective-permute-start(bf16[96,2176]{1,0:T(8,128)(2,1)} %slice.82), channel_id=1, source_target_pairs={{0,12},{1,13},{4,0},{5,1},{8,4},{9,5},{12,8},{13,9},{16,28},{17,29... | collective-permute-start | bytes 1253384 | tf_op jit(solution)/shard_map/ppermute | solution.py:38
  99.6 13.7 %collective-permute-start.2 = (bf16[96,2176]{1,0:T(8,128)(2,1)}, bf16[96,2176]{1,0:T(8,128)(2,1)S(1)}, u32[]{:S(2)}, u32[]{:S(2)}) collective-permute-start(bf16[96,2176]{1,0:T(8,128)(2,1)} %slice.81), channel_id=1, source_target_pairs={{0,4},{1,5},{4,8},{5,9},{8,12},{9,13},{12,0},{13,1},{16,20},{17,21... | collective-permute-start | bytes 1253384 | tf_op jit(solution)/shard_map/ppermute | solution.py:38
  113.4 1.8 copy-start
  128.0 5.3 %collective-permute-start.7 = (bf16[2,2,2,2,64,704]{5,4,3,2,1,0:T(8,128)(2,1)S(1)}, bf16[2,2,2,2,64,704]{5,4,3,2,1,0:T(8,128)(2,1)S(1)}, u32[]{:S(2)}, u32[]{:S(2)}) collective-permute-start(bf16[2,2,2,2,64,704]{5,4,3,2,1,0:T(8,128)(2,1)S(1)} %get-tuple-element.16), channel_id=1, source_target_pairs={{0,1},{1,0},{4,5},{5,4},{8,9},{9,8},{12,13},{13,12},{16,17},{17,16... | collective-permute-start | bytes 4325384 | tf_op jit(solution)/shard_map/ppermute | solution.py:38
  133.8 25.4 %collective-permute-start.8 = (bf16[2,2,2,64,704]{4,3,2,1,0:T(8,128)(2,1)S(1)}, bf16[2,2,2,64,704]{4,3,2,1,0:T(8,128)(2,1)S(1)}, u32[]{:S(2)}, u32[]{:S(2)}) collective-permute-start(bf16[2,2,2,64,704]{4,3,2,1,0:T(8,128)(2,1)S(1)} %get-tuple-element.27), channel_id=1, source_target_pairs={{0,16},{1,17},{4,20},{5,21},{8,24},{9,25},{12,28},{13,29},{16,0},{... | collective-permute-start | bytes 2162696 | tf_op jit(solution)/shard_map/ppermute | solution.py:38
  141.3 16.6 %all-to-all-start = ((bf16[4,48,2176]{2,1,0:T(8,128)(2,1)}), bf16[4,48,2176]{2,1,0:T(8,128)(2,1)S(1)}, u32[]{:S(2)}, u32[]{:S(2)}) async-start(bf16[4,48,2176]{2,1,0:T(8,128)(2,1)} %bitcast.15), calls=%async_computation | async-start | bytes 1671168 | tf_op jit(solution)/shard_map/all_to_all | solution.py:279
  159.2 44.7 %collective-permute-start.9 = (bf16[2,2,64,704]{3,2,1,0:T(8,128)(2,1)S(1)}, bf16[2,2,64,704]{3,2,1,0:T(8,128)(2,1)S(1)}, u32[]{:S(2)}, u32[]{:S(2)}) collective-permute-start(bf16[2,2,64,704]{3,2,1,0:T(8,128)(2,1)S(1)} %fusion.4), channel_id=1, source_target_pairs={{0,32},{1,33},{4,36},{5,37},{8,40},{9,41},{12,44},{13,45},{16,48},... | collective-permute-start | bytes 1081352 | tf_op jit(solution)/shard_map/ppermute | solution.py:38
  161.2 42.8 %collective-permute-start.6 = (bf16[24,2176]{1,0:T(8,128)(2,1)S(1)}, bf16[24,2176]{1,0:T(8,128)(2,1)S(1)}, u32[]{:S(2)}, u32[]{:S(2)}) collective-permute-start(bf16[24,2176]{1,0:T(8,128)(2,1)S(1)} %broadcast_select_fusion), channel_id=1, source_target_pairs={{0,2},{1,3},{4,6},{5,7},{8,10},{9,11},{12,14},{13,15},{16,18},{17,... | collective-permute-start | bytes 313352 | tf_op jit(solution)/shard_map/ppermute | solution.py:38
  205.6 7.2 %collective-permute-start.10 = (bf16[24,1024]{1,0:T(8,128)(2,1)S(1)}, bf16[24,1024]{1,0:T(8,128)(2,1)S(1)}, u32[]{:S(2)}, u32[]{:S(2)}) collective-permute-start(bf16[24,1024]{1,0:T(8,128)(2,1)S(1)} %get-tuple-element.30), channel_id=1, source_target_pairs={{0,768},{1,769},{4,772},{5,773},{8,776},{9,777},{12,780},{13,781},... | collective-permute-start | bytes 147464 | tf_op jit(solution)/shard_map/ppermute | solution.py:59

commit v4 on v3

--- a/solution.py
+++ b/solution.py
@@ -112,7 +112,7 @@
 
 
 def experts_kernel(
-    place_ref, line, left, right, far_left, far_right,
+    place_ref, line, early, left, right, far_left, far_right,
     up_own, down_own, up_other, down_other, back_out, keep_out, give_out,
     rows_ref, up_ref, down_ref, xs, gs, us, picked, metas, acts, hgs, result_ref, sums,
     landed, arrived, *, tok, feat, local, top,
@@ -121,12 +121,21 @@
     names = [place_ref[e].astype(F32) for e in range(experts)]
     block_at, y_at, spot = place_ref[experts], place_ref[experts + 1], place_ref[experts + 2]
     span = GROUPS * tok
+    head = early.shape[0] // Y
+    far = far_left.shape[0]
     landings = [
-        pltpu.make_async_copy(line, rows_ref.at[0], landed.at[0]),
-        pltpu.make_async_copy(left, rows_ref.at[1], landed.at[1]),
-        pltpu.make_async_copy(far_left, rows_ref.at[2, pl.ds(0, span)], landed.at[2]),
-        pltpu.make_async_copy(far_right, rows_ref.at[2, pl.ds(span, span)], landed.at[3]),
-        pltpu.make_async_copy(right, rows_ref.at[3], landed.at[4]),
+        (line, rows_ref.at[0]),
+        (left, rows_ref.at[1, pl.ds(head, left.shape[0])]),
+        (far_left, rows_ref.at[2, pl.ds(head, far)]),
+        (far_right, rows_ref.at[2, pl.ds(head + far, far_right.shape[0])]),
+        (right, rows_ref.at[3, pl.ds(head, right.shape[0])]),
+    ]
+    for d in range(1, Y):
+        start = pl.multiple_of(((y_at + Y - d) % Y) * head, head)
+        landings.append((early.at[pl.ds(start, head)], rows_ref.at[d, pl.ds(0, head)]))
+    landings = [
+        pltpu.make_async_copy(source, target, landed.at[i])
+        for i, (source, target) in enumerate(landings)
     ]
     copies = []
     for a, (up, down) in enumerate(((up_own, down_own), (up_other, down_other))):
@@ -227,7 +236,7 @@
             pltpu.VMEM((GROUPS * slots, units), BF16),
             pltpu.VMEM((rows, width), BF16),
             pltpu.VMEM((feat // GROUPS, units), BF16),
-            pltpu.SemaphoreType.DMA((len(pieces),)),
+            pltpu.SemaphoreType.DMA((len(pieces) + 2,)),
             pltpu.SemaphoreType.DMA((2, CORES)),
         ],
         compiler_params=pltpu.CompilerParams(vmem_limit_bytes=44 * 1024 * 1024),
@@ -265,14 +274,16 @@
     up_t, down = jnp.swapaxes(up_weight[0], 1, 2), down_weight[0]
 
     line = gather(mine, Z_CLASSES)
-    middle = line.shape[0] // 2
-    left, right = send(line, dy=1), send(line, dy=-1)
+    head = 2 * tok
+    early = gather(line[:head], Y_RINGS)
+    left, right = send(line[head:], dy=1), send(line[head:], dy=-1)
+    middle = (line.shape[0] - head) // 32 * 16 + 16
     far_left, far_right = send(left[:middle], dy=1), send(right[middle:], dy=-1)
     weights = [up_t, down]
     up_t, down, _ = lax.optimization_barrier((up_t, down, line))
     weights = weights + [send(up_t, flip=1), send(down, flip=1)]
     back, keep, give = run_experts(
-        [line, left, right, far_left, far_right], weights, where, tok, feat, top
+        [line, early, left, right, far_left, far_right], weights, where, tok, feat, top
     )
 
     share = back.shape[0] // Y
@@ -290,7 +301,7 @@
     keep = both_halves(keep[0], got[0])
     last = send(give, block_flip=2)
     beyond = send(outer, dz=Z_LO)
-    beyond, last = lax.optimization_barrier((beyond, last))
+    beyond, give = lax.optimization_barrier((beyond, give))
     added = inner.astype(F32) + beyond.astype(F32)
     dots = added[:, feat : feat + LANES]
     gate_grad = dots[:, :top] + dots[:, top : 2 * top]

time: 214 us -> 205 us (0.958)
  the two profiles are of different devices: /device:TPU:38 before, /device:TPU:24 now
where the time goes in v4:
time: 205 us; the launch traced here: 202 us
  blocking collectives  86.2 us (42%)
  waiting for transfers between devices  44.6 us (22%)
  starting transfers between devices  43.9 us (21%)
  Pallas kernels  13.8 us (7%)
  local copies, waits for them, and re-layouts  8.14 us (4%)
  other arithmetic  4.4 us (2%)
    all_gather x2, blocking collectives, gather(): lax.all_gather(block, PLANE, axis=0, tiled=True, axis_index_groups=rings)  86.2 us
    ppermute x10, waiting for transfers between devices, send(): return lax.ppermute(block, PLANE, moved(**route))  37.3 us
    ppermute x10, starting transfers between devices, send(): return lax.ppermute(block, PLANE, moved(**route))  33.5 us
    pallas_call x1, Pallas kernels, run_experts(): pl.pallas_call(functools.partial(experts_kernel, tok=tok, feat=feat, loca...  13.8 us
    all_to_all x1, waiting for transfers between devices, body(): lax.all_to_all(back, PLANE, 0, 0, tiled=True, axis_index_groups=Y_RINGS)  6.32 us
    ppermute x1, starting transfers between devices, send_to_section_before(): return lax.ppermute(block, ROUND, pairs)  5.87 us
    unnamed x12, local copies, waits for them, and re-layouts  5.69 us
    all_to_all x1, starting transfers between devices, body(): lax.all_to_all(back, PLANE, 0, 0, tiled=True, axis_index_groups=Y_RINGS)  4.52 us
  transfers between devices with their start and end apart: 12, of which 6 were waited for; matrix products, arithmetic and copies ran while one was open for 3% of the time, Pallas kernels for 0%

profile of v4, /device:TPU:24, one launch (start us, length us, event | category | flops | bytes accessed | tf_op | source)
XLA Modules:
  0.0 202.0 jit_solution(12355526912803759281)
XLA Ops:
  0.6 0.8 copy.13
  1.4 0.8 copy.14
  2.3 0.8 fusion.7
  3.1 67.5 %all_gather.6.line = bf16[192,2176]{1,0:T(8,128)(2,1)S(1)} all-gather(bf16[24,2176]{1,0:T(8,128)(2,1)S(1)} %fusion.7), channel_id=1, replica_groups={{0,64,128,192,2,66,130,194},{1,65,129,193,3,67,131,195},{4,68,132,196,6..., dimensions={0}, use_global_device_ids=true | all-gather | bytes 940032 | tf_op jit(solution)/shard_map/all_gather | solution.py:49
  70.6 1.9 collective-permute-start.4
  72.6 2.4 %collective-permute-start.5 = (bf16[2,704,1024]{2,1,0:T(8,128)(2,1)}, bf16[2,704,1024]{2,1,0:T(8,128)(2,1)}, u32[]{:S(2)}, u32[]{:S(2)}) collective-permute-start(bf16[2,704,1024]{2,1,0:T(8,128)(2,1)} %bitcast.48), channel_id=1, source_target_pairs={{0,1},{1,0},{4,5},{5,4},{8,9},{9,8},{12,13},{13,12},{16,17},{17,16... | collective-permute-start | bytes 8650760 | tf_op jit(solution)/shard_map/ppermute | solution.py:38
  75.0 1.9 collective-permute-start
  77.0 3.9 %collective-permute-start.1 = (bf16[144,2176]{1,0:T(8,128)(2,1)S(1)}, bf16[144,2176]{1,0:T(8,128)(2,1)S(1)}, u32[]{:S(2)}, u32[]{:S(2)}) collective-permute-start(bf16[144,2176]{1,0:T(8,128)(2,1)S(1)} %slice.91), channel_id=1, source_target_pairs={{0,12},{1,13},{4,0},{5,1},{8,4},{9,5},{12,8},{13,9},{16,28},{17,29... | collective-permute-start | bytes 1880072 | tf_op jit(solution)/shard_map/ppermute | solution.py:38
  80.9 12.1 %collective-permute-done.left = bf16[144,2176]{1,0:T(8,128)(2,1)S(1)} collective-permute-done((bf16[144,2176]{1,0:T(8,128)(2,1)S(1)}, bf16[144,2176]{1,0:T(8,128)(2,1)S(1)}, u32[]{:S(2)}, u32[]{:S(2)}) %collective-permute-start) | collective-permute-done | bytes 626720 | tf_op jit(solution)/shard_map/ppermute | solution.py:38
  93.0 0.8 slice.92
  93.7 3.4 %collective-permute-start.2 = (bf16[80,2176]{1,0:T(8,128)(2,1)}, bf16[80,2176]{1,0:T(8,128)(2,1)S(1)}, u32[]{:S(2)}, u32[]{:S(2)}) collective-permute-start(bf16[80,2176]{1,0:T(8,128)(2,1)} %slice.92), channel_id=1, source_target_pairs={{0,4},{1,5},{4,8},{5,9},{8,12},{9,13},{12,0},{13,1},{16,20},{17,21... | collective-permute-start | bytes 1044488 | tf_op jit(solution)/shard_map/ppermute | solution.py:38
  97.4 2.4 %collective-permute-start.3 = (bf16[64,2176]{1,0:T(8,128)(2,1)S(1)}, bf16[64,2176]{1,0:T(8,128)(2,1)S(1)}, u32[]{:S(2)}, u32[]{:S(2)}) collective-permute-start(bf16[64,2176]{1,0:T(8,128)(2,1)S(1)} %slice.93), channel_id=1, source_target_pairs={{0,12},{1,13},{4,0},{5,1},{8,4},{9,5},{12,8},{13,9},{16,28},{17,29... | collective-permute-start | bytes 835592 | tf_op jit(solution)/shard_map/ppermute | solution.py:38
  99.8 18.7 %all_gather.7.early = bf16[192,2176]{1,0:T(8,128)(2,1)S(1)} all-gather(bf16[48,2176]{1,0:T(8,128)(2,1)S(1)} %slice.90), channel_id=1, replica_groups={{0,4,8,12},{1,5,9,13},{16,20,24,28},{17,21,25,29},{32,36,40,44},{33,37,..., dimensions={0}, use_global_device_ids=true | all-gather | bytes 1044480 | tf_op jit(solution)/shard_map/all_gather | solution.py:49
  118.5 1.1 copy-done.1
  119.6 1.8 copy-done.2
  121.4 13.8 %shard_map.101 = (bf16[192,2176]{1,0:T(8,128)(2,1)}, bf16[2,2,2,2,64,704]{5,4,3,2,1,0:T(8,128)(2,1)S(1)}, bf16[2,2,2,2,64,704]{5,4,3,2,1,0:T(8,128)(2,1)}) custom-call(s32[7]{0:T(128)S(1)} %stack.31.place_ref, bf16[192,2176]{1,0:T(8,128)(2,1)S(1)} %all_gather.6.line, bf16[192,2176]{1,0:T(8,128)(2,1)S(1)} %all_gather.7.early, ...), custom_call_target="tpu_custom_call" | custom-call | flops 12000000000 | bytes 20000000 | tf_op jit(solution)/shard_map/pallas_call | solution.py:217
  135.2 1.9 collective-permute-start.7
  137.1 4.5 %all-to-all-start = ((bf16[4,48,2176]{2,1,0:T(8,128)(2,1)}), bf16[4,48,2176]{2,1,0:T(8,128)(2,1)S(1)}, u32[]{:S(2)}, u32[]{:S(2)}) async-start(bf16[4,48,2176]{2,1,0:T(8,128)(2,1)} %bitcast.15), calls=%async_computation | async-start | bytes 1671168 | tf_op jit(solution)/shard_map/all_to_all | solution.py:290
  141.7 3.0 %add_convert_fusion.1 = (bf16[1,2,2,2,64,704]{5,4,3,2,1,0:T(8,128)(2,1)}, bf16[2,2,2,64,704]{4,3,2,1,0:T(8,128)(2,1)}) fusion(bf16[2,2,2,2,64,704]{5,4,3,2,1,0:T(8,128)(2,1)} %collective-permute-done.7, bf16[2,2,2,2,64,704]{5,4,3,2,1,0:T(8,128)(2,1)S(1)} %get-tuple-element.14), kind=kLoop, calls=%fused_computation.1 | loop fusion | flops 2883584 | bytes 4325376 | tf_op jit(solution)/shard_map/convert_element_type | solution.py:250
  144.7 2.0 %collective-permute-start.8 = (bf16[2,2,2,64,704]{4,3,2,1,0:T(8,128)(2,1)}, bf16[2,2,2,64,704]{4,3,2,1,0:T(8,128)(2,1)S(1)}, u32[]{:S(2)}, u32[]{:S(2)}) collective-permute-start(bf16[2,2,2,64,704]{4,3,2,1,0:T(8,128)(2,1)} %get-tuple-element.25), channel_id=1, source_target_pairs={{0,16},{1,17},{4,20},{5,21},{8,24},{9,25},{12,28},{13,29},{16,0},{... | collective-permute-start | bytes 2162696 | tf_op jit(solution)/shard_map/ppermute | solution.py:38
  146.7 6.3 %all-to-all-done = bf16[4,48,2176]{2,1,0:T(8,128)(2,1)S(1)} async-done(((bf16[4,48,2176]{2,1,0:T(8,128)(2,1)}), bf16[4,48,2176]{2,1,0:T(8,128)(2,1)S(1)}, u32[]{:S(2)}, u32[]{:S(2)}) %all-to-all-start) | async-done | bytes 835616 | tf_op jit(solution)/shard_map/all_to_all | solution.py:290
  153.2 11.7 %collective-permute-start.6 = (bf16[24,2176]{1,0:T(8,128)(2,1)S(1)}, bf16[24,2176]{1,0:T(8,128)(2,1)S(1)}, u32[]{:S(2)}, u32[]{:S(2)}) collective-permute-start(bf16[24,2176]{1,0:T(8,128)(2,1)S(1)} %broadcast_select_fusion), channel_id=1, source_target_pairs={{0,2},{1,3},{4,6},{5,7},{8,10},{9,11},{12,14},{13,15},{16,18},{17,... | collective-permute-start | bytes 313352 | tf_op jit(solution)/shard_map/ppermute | solution.py:38
  164.9 14.1 %collective-permute-done.8 = bf16[2,2,2,64,704]{4,3,2,1,0:T(8,128)(2,1)S(1)} collective-permute-done((bf16[2,2,2,64,704]{4,3,2,1,0:T(8,128)(2,1)}, bf16[2,2,2,64,704]{4,3,2,1,0:T(8,128)(2,1)S(1)}, u32[]{:S(2)}, u32[]{:S(2)}) %collective-permute-start.8) | collective-permute-done | bytes 720928 | tf_op jit(solution)/shard_map/ppermute | solution.py:38
  179.1 1.9 collective-permute-start.10
  181.0 6.9 %collective-permute-done.6 = bf16[24,2176]{1,0:T(8,128)(2,1)S(1)} collective-permute-done((bf16[24,2176]{1,0:T(8,128)(2,1)S(1)}, bf16[24,2176]{1,0:T(8,128)(2,1)S(1)}, u32[]{:S(2)}, u32[]{:S(2)}) %collective-permute-start.6) | collective-permute-done | bytes 104480 | tf_op jit(solution)/shard_map/ppermute | solution.py:38
  187.9 0.6 fusion.12
  188.5 5.9 %collective-permute-start.9 = (bf16[24,1024]{1,0:T(8,128)(2,1)S(1)}, bf16[24,1024]{1,0:T(8,128)(2,1)S(1)}, u32[]{:S(2)}, u32[]{:S(2)}) collective-permute-start(bf16[24,1024]{1,0:T(8,128)(2,1)S(1)} %get-tuple-element.28), channel_id=1, source_target_pairs={{0,768},{1,769},{4,772},{5,773},{8,776},{9,777},{12,780},{13,781},... | collective-permute-start | bytes 147464 | tf_op jit(solution)/shard_map/ppermute | solution.py:59
  194.5 0.7 copy.15
  195.2 1.0 collective-permute-done.9
  196.2 4.3 %collective-permute-done.10 = bf16[2,2,64,704]{3,2,1,0:T(8,128)(2,1)S(1)} collective-permute-done((bf16[2,2,64,704]{3,2,1,0:T(8,128)(2,1)S(1)}, bf16[2,2,64,704]{3,2,1,0:T(8,128)(2,1)S(1)}, u32[]{:S(2)}, u32[]{:S(2)}) %collective-permute-start.10) | collective-permute-done | bytes 360480 | tf_op jit(solution)/shard_map/ppermute | solution.py:38
  200.6 0.8 fusion.11
  201.3 0.6 copy.17
  (26 shorter events, 0.9 us)
Async XLA Ops:
  70.6 47.8 %collective-permute-start.4 = (bf16[2,704,1024]{2,1,0:T(8,128)(2,1)}, bf16[2,704,1024]{2,1,0:T(8,128)(2,1)}, u32[]{:S(2)}, u32[]{:S(2)}) collective-permute-start(bf16[2,704,1024]{2,1,0:T(8,128)(2,1)} %bitcast.43), channel_id=1, source_target_pairs={{0,1},{1,0},{4,5},{5,4},{8,9},{9,8},{12,13},{13,12},{16,17},{17,16... | collective-permute-start | bytes 8650760 | tf_op jit(solution)/shard_map/ppermute | solution.py:38
  72.6 45.9 %collective-permute-start.5 = (bf16[2,704,1024]{2,1,0:T(8,128)(2,1)}, bf16[2,704,1024]{2,1,0:T(8,128)(2,1)}, u32[]{:S(2)}, u32[]{:S(2)}) collective-permute-start(bf16[2,704,1024]{2,1,0:T(8,128)(2,1)} %bitcast.48), channel_id=1, source_target_pairs={{0,1},{1,0},{4,5},{5,4},{8,9},{9,8},{12,13},{13,12},{16,17},{17,16... | collective-permute-start | bytes 8650760 | tf_op jit(solution)/shard_map/ppermute | solution.py:38
  75.0 17.9 %collective-permute-start = (bf16[144,2176]{1,0:T(8,128)(2,1)S(1)}, bf16[144,2176]{1,0:T(8,128)(2,1)S(1)}, u32[]{:S(2)}, u32[]{:S(2)}) collective-permute-start(bf16[144,2176]{1,0:T(8,128)(2,1)S(1)} %slice.91), channel_id=1, source_target_pairs={{0,4},{1,5},{4,8},{5,9},{8,12},{9,13},{12,0},{13,1},{16,20},{17,21... | collective-permute-start | bytes 1880072 | tf_op jit(solution)/shard_map/ppermute | solution.py:38
  77.0 20.4 %collective-permute-start.1 = (bf16[144,2176]{1,0:T(8,128)(2,1)S(1)}, bf16[144,2176]{1,0:T(8,128)(2,1)S(1)}, u32[]{:S(2)}, u32[]{:S(2)}) collective-permute-start(bf16[144,2176]{1,0:T(8,128)(2,1)S(1)} %slice.91), channel_id=1, source_target_pairs={{0,12},{1,13},{4,0},{5,1},{8,4},{9,5},{12,8},{13,9},{16,28},{17,29... | collective-permute-start | bytes 1880072 | tf_op jit(solution)/shard_map/ppermute | solution.py:38
  93.7 24.7 %collective-permute-start.2 = (bf16[80,2176]{1,0:T(8,128)(2,1)}, bf16[80,2176]{1,0:T(8,128)(2,1)S(1)}, u32[]{:S(2)}, u32[]{:S(2)}) collective-permute-start(bf16[80,2176]{1,0:T(8,128)(2,1)} %slice.92), channel_id=1, source_target_pairs={{0,4},{1,5},{4,8},{5,9},{8,12},{9,13},{12,0},{13,1},{16,20},{17,21... | collective-permute-start | bytes 1044488 | tf_op jit(solution)/shard_map/ppermute | solution.py:38
  97.3 21.1 %copy-start = (bf16[144,2176]{1,0:T(8,128)(2,1)}, bf16[144,2176]{1,0:T(8,128)(2,1)S(1)}, u32[]{:S(2)}) copy-start(bf16[144,2176]{1,0:T(8,128)(2,1)S(1)} %collective-permute-done.1.right) | copy-start | bytes 1880068
  97.4 21.1 %collective-permute-start.3 = (bf16[64,2176]{1,0:T(8,128)(2,1)S(1)}, bf16[64,2176]{1,0:T(8,128)(2,1)S(1)}, u32[]{:S(2)}, u32[]{:S(2)}) collective-permute-start(bf16[64,2176]{1,0:T(8,128)(2,1)S(1)} %slice.93), channel_id=1, source_target_pairs={{0,12},{1,13},{4,0},{5,1},{8,4},{9,5},{12,8},{13,9},{16,28},{17,29... | collective-permute-start | bytes 835592 | tf_op jit(solution)/shard_map/ppermute | solution.py:38
  118.5 1.1 copy-start.1
  119.6 1.8 copy-start.2
  135.2 6.4 %collective-permute-start.7 = (bf16[2,2,2,2,64,704]{5,4,3,2,1,0:T(8,128)(2,1)}, bf16[2,2,2,2,64,704]{5,4,3,2,1,0:T(8,128)(2,1)}, u32[]{:S(2)}, u32[]{:S(2)}) collective-permute-start(bf16[2,2,2,2,64,704]{5,4,3,2,1,0:T(8,128)(2,1)} %get-tuple-element.15), channel_id=1, source_target_pairs={{0,1},{1,0},{4,5},{5,4},{8,9},{9,8},{12,13},{13,12},{16,17},{17,16... | collective-permute-start | bytes 4325384 | tf_op jit(solution)/shard_map/ppermute | solution.py:38
  137.1 15.9 %all-to-all-start = ((bf16[4,48,2176]{2,1,0:T(8,128)(2,1)}), bf16[4,48,2176]{2,1,0:T(8,128)(2,1)S(1)}, u32[]{:S(2)}, u32[]{:S(2)}) async-start(bf16[4,48,2176]{2,1,0:T(8,128)(2,1)} %bitcast.15), calls=%async_computation | async-start | bytes 1671168 | tf_op jit(solution)/shard_map/all_to_all | solution.py:290
  144.7 34.3 %copy-start.3 = (bf16[1,2,2,2,64,704]{5,4,3,2,1,0:T(8,128)(2,1)S(1)}, bf16[1,2,2,2,64,704]{5,4,3,2,1,0:T(8,128)(2,1)}, u32[]{:S(2)}) copy-start(bf16[1,2,2,2,64,704]{5,4,3,2,1,0:T(8,128)(2,1)} %get-tuple-element.24) | copy-start | bytes 2162692
  144.7 34.3 %collective-permute-start.8 = (bf16[2,2,2,64,704]{4,3,2,1,0:T(8,128)(2,1)}, bf16[2,2,2,64,704]{4,3,2,1,0:T(8,128)(2,1)S(1)}, u32[]{:S(2)}, u32[]{:S(2)}) collective-permute-start(bf16[2,2,2,64,704]{4,3,2,1,0:T(8,128)(2,1)} %get-tuple-element.25), channel_id=1, source_target_pairs={{0,16},{1,17},{4,20},{5,21},{8,24},{9,25},{12,28},{13,29},{16,0},{... | collective-permute-start | bytes 2162696 | tf_op jit(solution)/shard_map/ppermute | solution.py:38
  153.2 34.6 %collective-permute-start.6 = (bf16[24,2176]{1,0:T(8,128)(2,1)S(1)}, bf16[24,2176]{1,0:T(8,128)(2,1)S(1)}, u32[]{:S(2)}, u32[]{:S(2)}) collective-permute-start(bf16[24,2176]{1,0:T(8,128)(2,1)S(1)} %broadcast_select_fusion), channel_id=1, source_target_pairs={{0,2},{1,3},{4,6},{5,7},{8,10},{9,11},{12,14},{13,15},{16,18},{17,... | collective-permute-start | bytes 313352 | tf_op jit(solution)/shard_map/ppermute | solution.py:38
  179.1 21.3 %collective-permute-start.10 = (bf16[2,2,64,704]{3,2,1,0:T(8,128)(2,1)S(1)}, bf16[2,2,64,704]{3,2,1,0:T(8,128)(2,1)S(1)}, u32[]{:S(2)}, u32[]{:S(2)}) collective-permute-start(bf16[2,2,64,704]{3,2,1,0:T(8,128)(2,1)S(1)} %fusion.4), channel_id=1, source_target_pairs={{0,32},{1,33},{4,36},{5,37},{8,40},{9,41},{12,44},{13,45},{16,48},... | collective-permute-start | bytes 1081352 | tf_op jit(solution)/shard_map/ppermute | solution.py:38
  188.5 7.6 %collective-permute-start.9 = (bf16[24,1024]{1,0:T(8,128)(2,1)S(1)}, bf16[24,1024]{1,0:T(8,128)(2,1)S(1)}, u32[]{:S(2)}, u32[]{:S(2)}) collective-permute-start(bf16[24,1024]{1,0:T(8,128)(2,1)S(1)} %get-tuple-element.28), channel_id=1, source_target_pairs={{0,768},{1,769},{4,772},{5,773},{8,776},{9,777},{12,780},{13,781},... | collective-permute-start | bytes 147464 | tf_op jit(solution)/shard_map/ppermute | solution.py:59

commit v5 on v4

--- a/solution.py
+++ b/solution.py
@@ -280,7 +280,7 @@
     middle = (line.shape[0] - head) // 32 * 16 + 16
     far_left, far_right = send(left[:middle], dy=1), send(right[middle:], dy=-1)
     weights = [up_t, down]
-    up_t, down, _ = lax.optimization_barrier((up_t, down, line))
+    up_t, down, *_ = lax.optimization_barrier((up_t, down, left, right))
     weights = weights + [send(up_t, flip=1), send(down, flip=1)]
     back, keep, give = run_experts(
         [line, early, left, right, far_left, far_right], weights, where, tok, feat, top

time: 205 us -> 204 us (level)
  waiting for transfers between devices: 44.6 us -> 40.9 us
  starting transfers between devices: 43.9 us -> 46.6 us
    ppermute x10, starting transfers between devices: 33.5 us -> 37.5 us  [send(): return lax.ppermute(block, PLANE, moved(**route))]
    ppermute x10, waiting for transfers between devices: 37.3 us -> 34.4 us  [send(): return lax.ppermute(block, PLANE, moved(**route))]
    unnamed x12 -> x10, local copies, waits for them, and re-layouts: 5.69 us -> 5.69 us
  transfers between devices with their start and end apart: 12 -> 12, of which waited for: 6 -> 7; matrix products, arithmetic and copies ran while one was open for 3% -> 2% of each run, Pallas kernels for 0% -> 0%
where the time goes in v5:
time: 204 us; the launch traced here: 201 us
  blocking collectives  87.2 us (43%)
  starting transfers between devices  46.6 us (23%)
  waiting for transfers between devices  40.9 us (20%)
  Pallas kernels  13.8 us (7%)
  local copies, waits for them, and re-layouts  7.38 us (4%)
  other arithmetic  4.11 us (2%)
    all_gather x2, blocking collectives, gather(): lax.all_gather(block, PLANE, axis=0, tiled=True, axis_index_groups=rings)  87.2 us
    ppermute x10, starting transfers between devices, send(): return lax.ppermute(block, PLANE, moved(**route))  37.5 us
    ppermute x10, waiting for transfers between devices, send(): return lax.ppermute(block, PLANE, moved(**route))  34.4 us
    pallas_call x1, Pallas kernels, run_experts(): pl.pallas_call(functools.partial(experts_kernel, tok=tok, feat=feat, loca...  13.8 us
    unnamed x10, local copies, waits for them, and re-layouts  5.69 us
    all_to_all x1, waiting for transfers between devices, body(): lax.all_to_all(back, PLANE, 0, 0, tiled=True, axis_index_groups=Y_RINGS)  5.57 us
    ppermute x1, starting transfers between devices, send_to_section_before(): return lax.ppermute(block, ROUND, pairs)  4.63 us
    all_to_all x1, starting transfers between devices, body(): lax.all_to_all(back, PLANE, 0, 0, tiled=True, axis_index_groups=Y_RINGS)  4.52 us
  transfers between devices with their start and end apart: 12, of which 7 were waited for; matrix products, arithmetic and copies ran while one was open for 2% of the time, Pallas kernels for 0%

profile of v5, /device:TPU:24, one launch (start us, length us, event | category | flops | bytes accessed | tf_op | source)
XLA Modules:
  0.0 201.0 jit_solution(14955560500803247944)
XLA Ops:
  0.6 0.8 copy.13
  1.4 0.8 copy.14
  2.3 0.8 fusion.7
  3.1 67.5 %all_gather.6.line = bf16[192,2176]{1,0:T(8,128)(2,1)S(1)} all-gather(bf16[24,2176]{1,0:T(8,128)(2,1)S(1)} %fusion.7), channel_id=1, replica_groups={{0,64,128,192,2,66,130,194},{1,65,129,193,3,67,131,195},{4,68,132,196,6..., dimensions={0}, use_global_device_ids=true | all-gather | bytes 940032 | tf_op jit(solution)/shard_map/all_gather | solution.py:49
  70.7 2.7 %collective-permute-start.1 = (bf16[144,2176]{1,0:T(8,128)(2,1)S(1)}, bf16[144,2176]{1,0:T(8,128)(2,1)S(1)}, u32[]{:S(2)}, u32[]{:S(2)}) collective-permute-start(bf16[144,2176]{1,0:T(8,128)(2,1)S(1)} %slice.91), channel_id=1, source_target_pairs={{0,12},{1,13},{4,0},{5,1},{8,4},{9,5},{12,8},{13,9},{16,28},{17,29... | collective-permute-start | bytes 1880072 | tf_op jit(solution)/shard_map/ppermute | solution.py:38
  73.3 4.4 %collective-permute-start = (bf16[144,2176]{1,0:T(8,128)(2,1)S(1)}, bf16[144,2176]{1,0:T(8,128)(2,1)S(1)}, u32[]{:S(2)}, u32[]{:S(2)}) collective-permute-start(bf16[144,2176]{1,0:T(8,128)(2,1)S(1)} %slice.91), channel_id=1, source_target_pairs={{0,4},{1,5},{4,8},{5,9},{8,12},{9,13},{12,0},{13,1},{16,20},{17,21... | collective-permute-start | bytes 1880072 | tf_op jit(solution)/shard_map/ppermute | solution.py:38
  77.8 6.3 %collective-permute-done.1.right = bf16[144,2176]{1,0:T(8,128)(2,1)S(1)} collective-permute-done((bf16[144,2176]{1,0:T(8,128)(2,1)S(1)}, bf16[144,2176]{1,0:T(8,128)(2,1)S(1)}, u32[]{:S(2)}, u32[]{:S(2)}) %collective-permute-start.1) | collective-permute-done | bytes 626720 | tf_op jit(solution)/shard_map/ppermute | solution.py:38
  84.1 1.5 collective-permute-done.left
  85.5 1.9 collective-permute-start.4
  87.4 2.4 %collective-permute-start.5 = (bf16[2,704,1024]{2,1,0:T(8,128)(2,1)}, bf16[2,704,1024]{2,1,0:T(8,128)(2,1)}, u32[]{:S(2)}, u32[]{:S(2)}) collective-permute-start(bf16[2,704,1024]{2,1,0:T(8,128)(2,1)} %bitcast.48), channel_id=1, source_target_pairs={{0,1},{1,0},{4,5},{5,4},{8,9},{9,8},{12,13},{13,12},{16,17},{17,16... | collective-permute-start | bytes 8650760 | tf_op jit(solution)/shard_map/ppermute | solution.py:38
  89.9 5.6 %collective-permute-start.2 = (bf16[80,2176]{1,0:T(8,128)(2,1)S(1)}, bf16[80,2176]{1,0:T(8,128)(2,1)S(1)}, u32[]{:S(2)}, u32[]{:S(2)}) collective-permute-start(bf16[80,2176]{1,0:T(8,128)(2,1)S(1)} %slice.92), channel_id=1, source_target_pairs={{0,4},{1,5},{4,8},{5,9},{8,12},{9,13},{12,0},{13,1},{16,20},{17,21... | collective-permute-start | bytes 1044488 | tf_op jit(solution)/shard_map/ppermute | solution.py:38
  95.7 1.9 collective-permute-start.3
  97.6 19.7 %all_gather.7.early = bf16[192,2176]{1,0:T(8,128)(2,1)S(1)} all-gather(bf16[48,2176]{1,0:T(8,128)(2,1)S(1)} %slice.90), channel_id=1, replica_groups={{0,4,8,12},{1,5,9,13},{16,20,24,28},{17,21,25,29},{32,36,40,44},{33,37,..., dimensions={0}, use_global_device_ids=true | all-gather | bytes 1044480 | tf_op jit(solution)/shard_map/all_gather | solution.py:49
  117.4 1.1 copy-done.1
  118.5 1.8 copy-done.2
  120.3 13.8 %shard_map.101 = (bf16[192,2176]{1,0:T(8,128)(2,1)}, bf16[2,2,2,2,64,704]{5,4,3,2,1,0:T(8,128)(2,1)S(1)}, bf16[2,2,2,2,64,704]{5,4,3,2,1,0:T(8,128)(2,1)}) custom-call(s32[7]{0:T(128)S(1)} %stack.31.place_ref, bf16[192,2176]{1,0:T(8,128)(2,1)S(1)} %all_gather.6.line, bf16[192,2176]{1,0:T(8,128)(2,1)S(1)} %all_gather.7.early, ...), custom_call_target="tpu_custom_call" | custom-call | flops 12000000000 | bytes 20000000 | tf_op jit(solution)/shard_map/pallas_call | solution.py:217
  134.1 1.9 collective-permute-start.7
  136.0 4.5 %all-to-all-start = ((bf16[4,48,2176]{2,1,0:T(8,128)(2,1)}), bf16[4,48,2176]{2,1,0:T(8,128)(2,1)S(1)}, u32[]{:S(2)}, u32[]{:S(2)}) async-start(bf16[4,48,2176]{2,1,0:T(8,128)(2,1)} %bitcast.15), calls=%async_computation | async-start | bytes 1671168 | tf_op jit(solution)/shard_map/all_to_all | solution.py:290
  140.5 2.7 %add_convert_fusion.1 = (bf16[1,2,2,2,64,704]{5,4,3,2,1,0:T(8,128)(2,1)S(1)}, bf16[2,2,2,64,704]{4,3,2,1,0:T(8,128)(2,1)}) fusion(bf16[2,2,2,2,64,704]{5,4,3,2,1,0:T(8,128)(2,1)} %collective-permute-done.7, bf16[2,2,2,2,64,704]{5,4,3,2,1,0:T(8,128)(2,1)S(1)} %get-tuple-element.14), kind=kLoop, calls=%fused_computation.1 | loop fusion | flops 2883584 | bytes 4325376 | tf_op jit(solution)/shard_map/convert_element_type | solution.py:250
  143.3 3.1 %collective-permute-start.8 = (bf16[2,2,2,64,704]{4,3,2,1,0:T(8,128)(2,1)}, bf16[2,2,2,64,704]{4,3,2,1,0:T(8,128)(2,1)S(1)}, u32[]{:S(2)}, u32[]{:S(2)}) collective-permute-start(bf16[2,2,2,64,704]{4,3,2,1,0:T(8,128)(2,1)} %get-tuple-element.25), channel_id=1, source_target_pairs={{0,16},{1,17},{4,20},{5,21},{8,24},{9,25},{12,28},{13,29},{16,0},{... | collective-permute-start | bytes 2162696 | tf_op jit(solution)/shard_map/ppermute | solution.py:38
  146.4 5.6 %all-to-all-done = bf16[4,48,2176]{2,1,0:T(8,128)(2,1)S(1)} async-done(((bf16[4,48,2176]{2,1,0:T(8,128)(2,1)}), bf16[4,48,2176]{2,1,0:T(8,128)(2,1)S(1)}, u32[]{:S(2)}, u32[]{:S(2)}) %all-to-all-start) | async-done | bytes 835616 | tf_op jit(solution)/shard_map/all_to_all | solution.py:290
  152.1 11.6 %collective-permute-start.6 = (bf16[24,2176]{1,0:T(8,128)(2,1)S(1)}, bf16[24,2176]{1,0:T(8,128)(2,1)S(1)}, u32[]{:S(2)}, u32[]{:S(2)}) collective-permute-start(bf16[24,2176]{1,0:T(8,128)(2,1)S(1)} %broadcast_select_fusion), channel_id=1, source_target_pairs={{0,2},{1,3},{4,6},{5,7},{8,10},{9,11},{12,14},{13,15},{16,18},{17,... | collective-permute-start | bytes 313352 | tf_op jit(solution)/shard_map/ppermute | solution.py:38
  163.8 14.7 %collective-permute-done.8 = bf16[2,2,2,64,704]{4,3,2,1,0:T(8,128)(2,1)S(1)} collective-permute-done((bf16[2,2,2,64,704]{4,3,2,1,0:T(8,128)(2,1)}, bf16[2,2,2,64,704]{4,3,2,1,0:T(8,128)(2,1)S(1)}, u32[]{:S(2)}, u32[]{:S(2)}) %collective-permute-start.8) | collective-permute-done | bytes 720928 | tf_op jit(solution)/shard_map/ppermute | solution.py:38
  178.5 1.9 collective-permute-start.10
  180.5 9.0 %collective-permute-done.6 = bf16[24,2176]{1,0:T(8,128)(2,1)S(1)} collective-permute-done((bf16[24,2176]{1,0:T(8,128)(2,1)S(1)}, bf16[24,2176]{1,0:T(8,128)(2,1)S(1)}, u32[]{:S(2)}, u32[]{:S(2)}) %collective-permute-start.6) | collective-permute-done | bytes 104480 | tf_op jit(solution)/shard_map/ppermute | solution.py:38
  189.5 0.6 fusion.12
  190.2 4.6 %collective-permute-start.9 = (bf16[24,1024]{1,0:T(8,128)(2,1)S(1)}, bf16[24,1024]{1,0:T(8,128)(2,1)S(1)}, u32[]{:S(2)}, u32[]{:S(2)}) collective-permute-start(bf16[24,1024]{1,0:T(8,128)(2,1)S(1)} %get-tuple-element.28), channel_id=1, source_target_pairs={{0,768},{1,769},{4,772},{5,773},{8,776},{9,777},{12,780},{13,781},... | collective-permute-start | bytes 147464 | tf_op jit(solution)/shard_map/ppermute | solution.py:59
  194.9 0.7 copy.15
  195.5 1.0 collective-permute-done.9
  196.5 2.9 %collective-permute-done.10 = bf16[2,2,64,704]{3,2,1,0:T(8,128)(2,1)S(1)} collective-permute-done((bf16[2,2,64,704]{3,2,1,0:T(8,128)(2,1)S(1)}, bf16[2,2,64,704]{3,2,1,0:T(8,128)(2,1)S(1)}, u32[]{:S(2)}, u32[]{:S(2)}) %collective-permute-start.10) | collective-permute-done | bytes 360480 | tf_op jit(solution)/shard_map/ppermute | solution.py:38
  199.6 0.8 fusion.11
  200.4 0.6 copy.17
  (24 shorter events, 0.9 us)
Async XLA Ops:
  70.7 13.4 %collective-permute-start.1 = (bf16[144,2176]{1,0:T(8,128)(2,1)S(1)}, bf16[144,2176]{1,0:T(8,128)(2,1)S(1)}, u32[]{:S(2)}, u32[]{:S(2)}) collective-permute-start(bf16[144,2176]{1,0:T(8,128)(2,1)S(1)} %slice.91), channel_id=1, source_target_pairs={{0,12},{1,13},{4,0},{5,1},{8,4},{9,5},{12,8},{13,9},{16,28},{17,29... | collective-permute-start | bytes 1880072 | tf_op jit(solution)/shard_map/ppermute | solution.py:38
  73.3 12.2 %collective-permute-start = (bf16[144,2176]{1,0:T(8,128)(2,1)S(1)}, bf16[144,2176]{1,0:T(8,128)(2,1)S(1)}, u32[]{:S(2)}, u32[]{:S(2)}) collective-permute-start(bf16[144,2176]{1,0:T(8,128)(2,1)S(1)} %slice.91), channel_id=1, source_target_pairs={{0,4},{1,5},{4,8},{5,9},{8,12},{9,13},{12,0},{13,1},{16,20},{17,21... | collective-permute-start | bytes 1880072 | tf_op jit(solution)/shard_map/ppermute | solution.py:38
  84.1 33.3 %copy-start = (bf16[144,2176]{1,0:T(8,128)(2,1)}, bf16[144,2176]{1,0:T(8,128)(2,1)S(1)}, u32[]{:S(2)}) copy-start(bf16[144,2176]{1,0:T(8,128)(2,1)S(1)} %collective-permute-done.1.right) | copy-start | bytes 1880068
  85.5 31.8 %collective-permute-start.4 = (bf16[2,704,1024]{2,1,0:T(8,128)(2,1)}, bf16[2,704,1024]{2,1,0:T(8,128)(2,1)}, u32[]{:S(2)}, u32[]{:S(2)}) collective-permute-start(bf16[2,704,1024]{2,1,0:T(8,128)(2,1)} %bitcast.43), channel_id=1, source_target_pairs={{0,1},{1,0},{4,5},{5,4},{8,9},{9,8},{12,13},{13,12},{16,17},{17,16... | collective-permute-start | bytes 8650760 | tf_op jit(solution)/shard_map/ppermute | solution.py:38
  87.4 29.9 %collective-permute-start.5 = (bf16[2,704,1024]{2,1,0:T(8,128)(2,1)}, bf16[2,704,1024]{2,1,0:T(8,128)(2,1)}, u32[]{:S(2)}, u32[]{:S(2)}) collective-permute-start(bf16[2,704,1024]{2,1,0:T(8,128)(2,1)} %bitcast.48), channel_id=1, source_target_pairs={{0,1},{1,0},{4,5},{5,4},{8,9},{9,8},{12,13},{13,12},{16,17},{17,16... | collective-permute-start | bytes 8650760 | tf_op jit(solution)/shard_map/ppermute | solution.py:38
  89.9 27.4 %collective-permute-start.2 = (bf16[80,2176]{1,0:T(8,128)(2,1)S(1)}, bf16[80,2176]{1,0:T(8,128)(2,1)S(1)}, u32[]{:S(2)}, u32[]{:S(2)}) collective-permute-start(bf16[80,2176]{1,0:T(8,128)(2,1)S(1)} %slice.92), channel_id=1, source_target_pairs={{0,4},{1,5},{4,8},{5,9},{8,12},{9,13},{12,0},{13,1},{16,20},{17,21... | collective-permute-start | bytes 1044488 | tf_op jit(solution)/shard_map/ppermute | solution.py:38
  95.7 21.6 %collective-permute-start.3 = (bf16[64,2176]{1,0:T(8,128)(2,1)S(1)}, bf16[64,2176]{1,0:T(8,128)(2,1)S(1)}, u32[]{:S(2)}, u32[]{:S(2)}) collective-permute-start(bf16[64,2176]{1,0:T(8,128)(2,1)S(1)} %slice.93), channel_id=1, source_target_pairs={{0,12},{1,13},{4,0},{5,1},{8,4},{9,5},{12,8},{13,9},{16,28},{17,29... | collective-permute-start | bytes 835592 | tf_op jit(solution)/shard_map/ppermute | solution.py:38
  117.4 1.1 copy-start.1
  118.5 1.8 copy-start.2
  134.1 6.4 %collective-permute-start.7 = (bf16[2,2,2,2,64,704]{5,4,3,2,1,0:T(8,128)(2,1)}, bf16[2,2,2,2,64,704]{5,4,3,2,1,0:T(8,128)(2,1)}, u32[]{:S(2)}, u32[]{:S(2)}) collective-permute-start(bf16[2,2,2,2,64,704]{5,4,3,2,1,0:T(8,128)(2,1)} %get-tuple-element.15), channel_id=1, source_target_pairs={{0,1},{1,0},{4,5},{5,4},{8,9},{9,8},{12,13},{13,12},{16,17},{17,16... | collective-permute-start | bytes 4325384 | tf_op jit(solution)/shard_map/ppermute | solution.py:38
  136.0 15.9 %all-to-all-start = ((bf16[4,48,2176]{2,1,0:T(8,128)(2,1)}), bf16[4,48,2176]{2,1,0:T(8,128)(2,1)S(1)}, u32[]{:S(2)}, u32[]{:S(2)}) async-start(bf16[4,48,2176]{2,1,0:T(8,128)(2,1)} %bitcast.15), calls=%async_computation | async-start | bytes 1671168 | tf_op jit(solution)/shard_map/all_to_all | solution.py:290
  143.3 35.2 %collective-permute-start.8 = (bf16[2,2,2,64,704]{4,3,2,1,0:T(8,128)(2,1)}, bf16[2,2,2,64,704]{4,3,2,1,0:T(8,128)(2,1)S(1)}, u32[]{:S(2)}, u32[]{:S(2)}) collective-permute-start(bf16[2,2,2,64,704]{4,3,2,1,0:T(8,128)(2,1)} %get-tuple-element.25), channel_id=1, source_target_pairs={{0,16},{1,17},{4,20},{5,21},{8,24},{9,25},{12,28},{13,29},{16,0},{... | collective-permute-start | bytes 2162696 | tf_op jit(solution)/shard_map/ppermute | solution.py:38
  152.1 37.4 %collective-permute-start.6 = (bf16[24,2176]{1,0:T(8,128)(2,1)S(1)}, bf16[24,2176]{1,0:T(8,128)(2,1)S(1)}, u32[]{:S(2)}, u32[]{:S(2)}) collective-permute-start(bf16[24,2176]{1,0:T(8,128)(2,1)S(1)} %broadcast_select_fusion), channel_id=1, source_target_pairs={{0,2},{1,3},{4,6},{5,7},{8,10},{9,11},{12,14},{13,15},{16,18},{17,... | collective-permute-start | bytes 313352 | tf_op jit(solution)/shard_map/ppermute | solution.py:38
  178.5 20.9 %collective-permute-start.10 = (bf16[2,2,64,704]{3,2,1,0:T(8,128)(2,1)S(1)}, bf16[2,2,64,704]{3,2,1,0:T(8,128)(2,1)S(1)}, u32[]{:S(2)}, u32[]{:S(2)}) collective-permute-start(bf16[2,2,64,704]{3,2,1,0:T(8,128)(2,1)S(1)} %fusion.4), channel_id=1, source_target_pairs={{0,32},{1,33},{4,36},{5,37},{8,40},{9,41},{12,44},{13,45},{16,48},... | collective-permute-start | bytes 1081352 | tf_op jit(solution)/shard_map/ppermute | solution.py:38
  190.2 6.4 %collective-permute-start.9 = (bf16[24,1024]{1,0:T(8,128)(2,1)S(1)}, bf16[24,1024]{1,0:T(8,128)(2,1)S(1)}, u32[]{:S(2)}, u32[]{:S(2)}) collective-permute-start(bf16[24,1024]{1,0:T(8,128)(2,1)S(1)} %get-tuple-element.28), channel_id=1, source_target_pairs={{0,768},{1,769},{4,772},{5,773},{8,776},{9,777},{12,780},{13,781},... | collective-permute-start | bytes 147464 | tf_op jit(solution)/shard_map/ppermute | solution.py:59
